TPU v7x, 32 devices: a whole 2x2x4 slice. The times are simulated.
32 devices in a mesh: gx: 16 (over z, y, core), gy: 2 (over x).
Axes of the slice: x: 2, y: 2, z: 4, core: 2. Of those that a mesh axis runs over, the one named last changes fastest.
Arguments:
- moisture: float32 [2048, 20, 128], P(('gx', 'gy')), may hold values from 0.05 to 1
- diffusivity: float32 [2048, 20, 128], P(('gx', 'gy')), may hold values from 0.1 to 4
- rain: float32 [2048, 128], P(('gx', 'gy')), may hold values from 0 to 2
- head: float32 [50, 256, 256], P(None, 'gx', 'gy'), may hold values from -4 to 4
- conductivity: float32 [50, 256, 256], P(None, 'gx', 'gy'), may hold values from 0.05 to 1
- tile_ids: int32 [2048], P(('gx', 'gy')), may hold values from 0 to 1, as said below
- offsets: int32 [2048], P(('gx', 'gy')), may hold values from 0 to 15
- patch_ids: int32 [2048], P(('gx', 'gy')), may hold values from 0 to 7
- counts: int32 [32], P(('gx', 'gy')), may hold values from 48 to 64, as said below
Outputs:
- head_out: float32 [50, 256, 256], P(None, 'gx', 'gy')
- moisture_out: float32 [2048, 20, 128], P(('gx', 'gy'))
- patch_sums: float32 [256, 128], P(('gx', 'gy'))
Inputs may be any that keep to these rules, and one draw needn't show every extreme that they name: `tile_ids`: only the first counts[d] block slots of device d are used; the others' entries are arbitrary. Among the used blocks of one device at most 32 name the same tile, and in every gx row one tile is named by exactly 32 used blocks of every device of that row. `counts`: some device uses all 64 slots in every draw.
All inputs are finite; a program needn't handle non-finite values.
Results may differ from a plain program's by a relative error of at most 0.00016.
Values sent between devices are 32-bit elements; how exact they have to be, the bound alone decides.
A program may use at most 64 MiB of HBM per device.

v0:
```python
import jax
import jax.numpy as jnp
from jax import lax
from jax.sharding import PartitionSpec as P

PATCH_DEV = 8
SWEEPS = 6


flow_rate = 0.15
capillary = 0.5


def with_halo(cells, sides, width):
    for axis, dim in sides:
        count = lax.axis_size(axis)
        ends = count - 1
        head = lax.slice_in_dim(cells, 0, width, axis=dim)
        tail = lax.slice_in_dim(cells, cells.shape[dim] - width, cells.shape[dim], axis=dim)
        cells = jnp.concatenate(
            [
                lax.ppermute(tail, axis, [(i, (i + 1) % count) for i in range(ends)]),
                cells,
                lax.ppermute(head, axis, [((i + 1) % count, i) for i in range(ends)]),
            ],
            axis=dim,
        )
    return cells


def column_solve(moisture, diffusivity, rain):
    depth = moisture.shape[1]
    ratios = []
    forward_vals = []
    for layer_k in range(depth):
        lower_coef = diffusivity[:, layer_k, :]
        source = moisture[:, layer_k, :]
        if layer_k == 0:
            source = source + rain
            pivot = 1.0 + lower_coef
            carried = source / pivot
        else:
            upper_coef = diffusivity[:, layer_k - 1, :]
            pivot = 1.0 + lower_coef + upper_coef - upper_coef * ratios[-1]
            carried = (source + upper_coef * forward_vals[-1]) / pivot
        ratios.append(lower_coef / pivot)
        forward_vals.append(carried)
    solved = [forward_vals[-1]]
    for layer_k in range(depth - 2, -1, -1):
        solved.append(forward_vals[layer_k] + ratios[layer_k] * solved[-1])
    return jnp.stack(solved[::-1], axis=1)


def lateral_core(padded_head, padded_cond):
    inner_rows = padded_head.shape[1] - 2
    inner_cols = padded_head.shape[2] - 2
    centre = padded_head[:, 1:-1, 1:-1]
    centre_cond = padded_cond[:, 1:-1, 1:-1]
    flux_total = jnp.zeros_like(centre)
    for row_shift, col_shift in ((0, 1), (2, 1), (1, 0), (1, 2)):
        beside = padded_head[
            :, row_shift : row_shift + inner_rows, col_shift : col_shift + inner_cols
        ]
        beside_cond = padded_cond[
            :, row_shift : row_shift + inner_rows, col_shift : col_shift + inner_cols
        ]
        flux_total = flux_total + 0.5 * (centre_cond + beside_cond) * (beside - centre)
    vertical = 0.5 * (centre_cond[1:] + centre_cond[:-1]) * (centre[1:] - centre[:-1])
    flux_total = (
        flux_total
        + jnp.pad(vertical, ((0, 1), (0, 0), (0, 0)))
        - jnp.pad(vertical, ((1, 0), (0, 0), (0, 0)))
    )
    return centre + flow_rate * flux_total


def local(moisture, diffusivity, rain, head, conductivity, tile_ids, offsets, patch_ids, counts):
    highest = lax.Precision.HIGHEST
    block_count = moisture.shape[0]
    tile_count = lax.axis_size("gy")
    capacity = block_count // 2
    tile_rows = head.shape[1]
    tile_cols = head.shape[2]
    wet = column_solve(moisture, diffusivity, rain)
    bottom = wet[:, -1, :]
    drain = diffusivity[:, -1, :] * bottom
    in_use = jnp.arange(block_count, dtype=jnp.int32) < counts[0]
    in_use_f = in_use.astype(jnp.float32)
    to_tile = (
        (tile_ids[:, None] == jnp.arange(tile_count, dtype=jnp.int32)[None, :]) & in_use[:, None]
    ).astype(jnp.int32)
    before = jnp.cumsum(to_tile, axis=0) - to_tile
    slot_of = jnp.sum(before * to_tile, axis=1)
    slot_match = slot_of[None, None, :] == jnp.arange(capacity, dtype=jnp.int32)[None, :, None]
    placing = (to_tile.T[:, None, :] * slot_match).astype(jnp.float32)
    outgoing = jnp.einsum("tcb,bj->tcj", placing, drain, precision=highest)
    out_rows = (
        jnp.einsum("tcb,b->tc", placing, (offsets + 1).astype(jnp.float32), precision=highest) - 1.0
    )
    incoming, in_rows = (
        lax.all_to_all(outgoing, "gy", split_axis=0, concat_axis=0, tiled=True),
        lax.all_to_all(out_rows, "gy", split_axis=0, concat_axis=0, tiled=True),
    )
    slot_total = tile_count * capacity
    landing = (
        in_rows.reshape(1, slot_total) == jnp.arange(tile_rows, dtype=jnp.float32)[:, None]
    ).astype(jnp.float32)
    recharge = jnp.dot(landing, incoming.reshape(slot_total, tile_cols), precision=highest)
    field = head.at[0].add(recharge)
    padded_cond = with_halo(conductivity, (("gx", 1), ("gy", 2)), 1)
    for sweep_k in range(SWEEPS):
        padded_head = with_halo(field, (("gx", 1), ("gy", 2)), 1)
        field = lateral_core(padded_head, padded_cond)
    surface = field[0]
    answered = jnp.dot(landing.T, surface, precision=highest).reshape(
        tile_count, capacity, tile_cols
    )
    returned = lax.all_to_all(answered, "gy", split_axis=0, concat_axis=0, tiled=True)
    saturation = jnp.einsum("tcb,tcj->bj", placing, returned, precision=highest)
    new_bottom = bottom + capillary * (saturation - in_use_f[:, None] * bottom)
    moisture_out = wet.at[:, -1, :].set(new_bottom)
    patch_hot = (patch_ids[None, :] == jnp.arange(PATCH_DEV, dtype=jnp.int32)[:, None]).astype(
        jnp.float32
    )
    patch_sums = jnp.dot(patch_hot, saturation, precision=highest)
    return (field, moisture_out, patch_sums)


def solution(mesh):
    placed = (
        P(("gx", "gy"), None, None),
        P(("gx", "gy"), None, None),
        P(("gx", "gy"), None),
        P(None, "gx", "gy"),
        P(None, "gx", "gy"),
        P(("gx", "gy")),
        P(("gx", "gy")),
        P(("gx", "gy")),
        P(("gx", "gy")),
    )
    return jax.shard_map(
        local,
        mesh=mesh,
        in_specs=placed,
        out_specs=(P(None, "gx", "gy"), P(("gx", "gy"), None, None), P(("gx", "gy"), None)),
        check_vma=False,
    )
```

profile of v0, /device:TPU:24, one launch (start us, length us, event | category | flops | bytes accessed | tf_op | source)
XLA Modules:
  0.0 166.1 jit_solution(10259831627841065971)
XLA Ops:
  3.8 0.9 fusion.167
  5.2 3.2 %all-to-all-start = ((f32[2,1,32]{2,1,0:T(1,128)}), f32[2,1,32]{2,1,0:T(1,128)S(1)}, u32[]{:S(2)}, u32[]{:S(2)}) async-start(f32[2,1,32]{2,1,0:T(1,128)} %bitcast.5), calls=%async_computation | async-start | bytes 2048 | tf_op jit(solution)/shard_map/all_to_all | solution.py:102
  8.5 2.8 %collective-permute-start.2 = (f32[50,1,128]{2,1,0:T(1,128)S(1)}, f32[50,1,128]{2,1,0:T(1,128)S(1)}, u32[]{:S(2)}, u32[]{:S(2)}) collective-permute-start(f32[50,1,128]{2,1,0:T(1,128)S(1)} %get-tuple-element.103), channel_id=1, source_target_pairs={{2,0},{4,2},{6,4},{8,6},{10,8},{12,10},{14,12},{16,14},{18,16},{20... | collective-permute-start | bytes 76808 | tf_op jit(solution)/shard_map/ppermute | solution.py:24
  11.3 1.9 %collective-permute-start = (f32[50,1,128]{2,1,0:T(1,128)S(1)}, f32[50,1,128]{2,1,0:T(1,128)S(1)}, u32[]{:S(2)}, u32[]{:S(2)}) collective-permute-start(f32[50,1,128]{2,1,0:T(1,128)S(1)} %get-tuple-element.104), channel_id=1, source_target_pairs={{0,2},{2,4},{4,6},{6,8},{8,10},{10,12},{12,14},{14,16},{16,18},{18... | collective-permute-start | bytes 76808 | tf_op jit(solution)/shard_map/ppermute | solution.py:22
  13.2 1.3 fusion.157
  15.1 1.5 constant_dynamic-update-slice_fusion.19
  18.0 3.3 %all-to-all-start.1 = ((f32[2,32,128]{2,1,0:T(8,128)}), f32[2,32,128]{2,1,0:T(8,128)S(1)}, u32[]{:S(2)}, u32[]{:S(2)}) async-start(f32[2,32,128]{2,1,0:T(8,128)} %fusion.106), calls=%async_computation.1 | async-start | bytes 65536 | tf_op jit(solution)/shard_map/all_to_all | solution.py:101
  22.7 2.7 %all-to-all-done.1 = f32[2,32,128]{2,1,0:T(8,128)S(1)} async-done(((f32[2,32,128]{2,1,0:T(8,128)}), f32[2,32,128]{2,1,0:T(8,128)S(1)}, u32[]{:S(2)}, u32[]{:S(2)}) %all-to-all-start.1) | async-done | bytes 32800 | tf_op jit(solution)/shard_map/all_to_all | solution.py:101
  25.5 2.0 %collective-permute-start.1 = (f32[50,1,128]{2,1,0:T(1,128)S(1)}, f32[50,1,128]{2,1,0:T(1,128)S(1)}, u32[]{:S(2)}, u32[]{:S(2)}) collective-permute-start(f32[50,1,128]{2,1,0:T(1,128)S(1)} %get-tuple-element.105), channel_id=1, source_target_pairs={{0,2},{2,4},{4,6},{6,8},{8,10},{10,12},{12,14},{14,16},{16,18},{18... | collective-permute-start | bytes 76808 | tf_op jit(solution)/shard_map/ppermute | solution.py:22
  27.6 4.4 %collective-permute-start.3 = (f32[50,1,128]{2,1,0:T(1,128)S(1)}, f32[50,1,128]{2,1,0:T(1,128)S(1)}, u32[]{:S(2)}, u32[]{:S(2)}) collective-permute-start(f32[50,1,128]{2,1,0:T(1,128)S(1)} %get-tuple-element.106), channel_id=1, source_target_pairs={{2,0},{4,2},{6,4},{8,6},{10,8},{12,10},{14,12},{16,14},{18,16},{20... | collective-permute-start | bytes 76808 | tf_op jit(solution)/shard_map/ppermute | solution.py:24
  33.0 1.9 %collective-permute-start.4 = (f32[50,18,1]{0,1,2:T(8,128)S(1)}, f32[50,18,1]{0,1,2:T(8,128)S(1)}, u32[]{:S(2)}, u32[]{:S(2)}) collective-permute-start(f32[50,18,1]{0,1,2:T(8,128)S(1)} %copy.13), channel_id=1, source_target_pairs={{0,1},{2,3},{4,5},{6,7},{8,9},{10,11},{12,13},{14,15},{16,17},{18,... | collective-permute-start | bytes 10808 | tf_op jit(solution)/shard_map/ppermute | solution.py:22
  34.9 1.3 collective-permute-start.6
  37.7 1.3 collective-permute-start.7
  39.0 4.5 %collective-permute-start.5 = (f32[50,18,1]{0,1,2:T(8,128)S(1)}, f32[50,18,1]{0,1,2:T(8,128)S(1)}, u32[]{:S(2)}, u32[]{:S(2)}) collective-permute-start(f32[50,18,1]{0,1,2:T(8,128)S(1)} %copy.15), channel_id=1, source_target_pairs={{0,1},{2,3},{4,5},{6,7},{8,9},{10,11},{12,13},{14,15},{16,17},{18,... | collective-permute-start | bytes 10808 | tf_op jit(solution)/shard_map/ppermute | solution.py:22
  44.0 1.2 copy.14
  45.2 1.2 copy.16
  46.3 1.2 copy.20
  47.5 2.6 %fusion.83 = (f32[50,16,128]{2,1,0:T(8,128)S(1)}, f32[50,16,128]{2,1,0:T(8,128)S(1)}, f32[50,16,128]{2,1,0:T(8,128)S(1)}) fusion(f32[50,16,128]{2,1,0:T(8,128)S(1)} %fusion.1, f32[50,18,1]{2,1,0:T(8,128)} %copy.20, f32[50,1,128]{2,1,0:T(1,128)} %copy-done.28, f32[50,1,128]{2,1,0:T(1,128)} %copy-done.27, f32[50,18,1]{2,1,0:T(8,128)} %copy.16, ...), kind=kLoop, calls=%fused_computation.133 | loop fusion | flops 3993600 | bytes 2566208 | tf_op jit(solution)/shard_map/add | solution.py:74
  50.2 1.9 %collective-permute-start.8 = (f32[50,1,128]{2,1,0:T(1,128)S(1)}, f32[50,1,128]{2,1,0:T(1,128)S(1)}, u32[]{:S(2)}, u32[]{:S(2)}) collective-permute-start(f32[50,1,128]{2,1,0:T(1,128)S(1)} %get-tuple-element.101), channel_id=1, source_target_pairs={{0,2},{2,4},{4,6},{6,8},{8,10},{10,12},{12,14},{14,16},{16,18},{18... | collective-permute-start | bytes 76808 | tf_op jit(solution)/shard_map/ppermute | solution.py:22
  52.1 4.5 %collective-permute-start.9 = (f32[50,1,128]{2,1,0:T(1,128)S(1)}, f32[50,1,128]{2,1,0:T(1,128)S(1)}, u32[]{:S(2)}, u32[]{:S(2)}) collective-permute-start(f32[50,1,128]{2,1,0:T(1,128)S(1)} %get-tuple-element.102), channel_id=1, source_target_pairs={{2,0},{4,2},{6,4},{8,6},{10,8},{12,10},{14,12},{16,14},{18,16},{20... | collective-permute-start | bytes 76808 | tf_op jit(solution)/shard_map/ppermute | solution.py:24
  57.3 0.9 collective-permute-done.9
  58.8 1.1 fusion.228
  59.8 1.4 copy.21
  61.5 1.3 collective-permute-start.11
  62.8 4.5 %collective-permute-start.10 = (f32[50,18,1]{0,1,2:T(8,128)S(1)}, f32[50,18,1]{0,1,2:T(8,128)S(1)}, u32[]{:S(2)}, u32[]{:S(2)}) collective-permute-start(f32[50,18,1]{0,1,2:T(8,128)S(1)} %copy.21), channel_id=1, source_target_pairs={{0,1},{2,3},{4,5},{6,7},{8,9},{10,11},{12,13},{14,15},{16,17},{18,... | collective-permute-start | bytes 10808 | tf_op jit(solution)/shard_map/ppermute | solution.py:22
  67.5 1.3 collective-permute-done.10
  69.1 1.2 copy.24
  70.3 1.8 %fusion.68 = f32[50,16,128]{2,1,0:T(8,128)S(1)} fusion(f32[50,16,128]{2,1,0:T(8,128)S(1)} %get-tuple-element.40, f32[50,16,128]{2,1,0:T(8,128)S(1)} %get-tuple-element.42, f32[50,18,1]{2,1,0:T(8,128)} %copy.24, f32[50,1,128]{2,1,0:T(1,128)} %copy-done.23, f32[50,1,128]{2,1,0:T(1,128)} %copy-done.19, f32[50,16,128]{2,1,0:T(8,128)S(1)} %get-tuple-element.41, ...), kind=kLoop, calls=%fused_computation.110 | loop fusion | flops 2969600 | bytes 2559008 | tf_op jit(solution)/shard_map/add | solution.py:74
  72.2 1.9 %collective-permute-start.12 = (f32[50,1,128]{2,1,0:T(1,128)S(1)}, f32[50,1,128]{2,1,0:T(1,128)S(1)}, u32[]{:S(2)}, u32[]{:S(2)}) collective-permute-start(f32[50,1,128]{2,1,0:T(1,128)S(1)} %get-tuple-element.99), channel_id=1, source_target_pairs={{0,2},{2,4},{4,6},{6,8},{8,10},{10,12},{12,14},{14,16},{16,18},{18... | collective-permute-start | bytes 76808 | tf_op jit(solution)/shard_map/ppermute | solution.py:22
  74.1 4.5 %collective-permute-start.13 = (f32[50,1,128]{2,1,0:T(1,128)S(1)}, f32[50,1,128]{2,1,0:T(1,128)S(1)}, u32[]{:S(2)}, u32[]{:S(2)}) collective-permute-start(f32[50,1,128]{2,1,0:T(1,128)S(1)} %get-tuple-element.100), channel_id=1, source_target_pairs={{2,0},{4,2},{6,4},{8,6},{10,8},{12,10},{14,12},{16,14},{18,16},{20... | collective-permute-start | bytes 76808 | tf_op jit(solution)/shard_map/ppermute | solution.py:24
  79.4 0.8 collective-permute-done.13
  81.8 1.3 collective-permute-start.15
  83.1 4.5 %collective-permute-start.14 = (f32[50,18,1]{0,1,2:T(8,128)S(1)}, f32[50,18,1]{0,1,2:T(8,128)S(1)}, u32[]{:S(2)}, u32[]{:S(2)}) collective-permute-start(f32[50,18,1]{0,1,2:T(8,128)S(1)} %copy.25), channel_id=1, source_target_pairs={{0,1},{2,3},{4,5},{6,7},{8,9},{10,11},{12,13},{14,15},{16,17},{18,... | collective-permute-start | bytes 10808 | tf_op jit(solution)/shard_map/ppermute | solution.py:22
  87.7 1.3 collective-permute-done.14
  89.4 1.2 copy.28
  90.6 1.8 %fusion.53 = f32[50,16,128]{2,1,0:T(8,128)S(1)} fusion(f32[50,16,128]{2,1,0:T(8,128)S(1)} %fusion.68, f32[50,16,128]{2,1,0:T(8,128)S(1)} %get-tuple-element.42, f32[50,18,1]{2,1,0:T(8,128)} %copy.28, f32[50,1,128]{2,1,0:T(1,128)} %copy-done.25, f32[50,1,128]{2,1,0:T(1,128)} %copy-done.21, f32[50,16,128]{2,1,0:T(8,128)S(1)} %get-tuple-element.41, ...), kind=kLoop, calls=%fused_computation.87 | loop fusion | flops 2969600 | bytes 2559008 | tf_op jit(solution)/shard_map/add | solution.py:74
  92.4 1.9 %collective-permute-start.16 = (f32[50,1,128]{2,1,0:T(1,128)S(1)}, f32[50,1,128]{2,1,0:T(1,128)S(1)}, u32[]{:S(2)}, u32[]{:S(2)}) collective-permute-start(f32[50,1,128]{2,1,0:T(1,128)S(1)} %get-tuple-element.97), channel_id=1, source_target_pairs={{0,2},{2,4},{4,6},{6,8},{8,10},{10,12},{12,14},{14,16},{16,18},{18... | collective-permute-start | bytes 76808 | tf_op jit(solution)/shard_map/ppermute | solution.py:22
  94.4 4.5 %collective-permute-start.17 = (f32[50,1,128]{2,1,0:T(1,128)S(1)}, f32[50,1,128]{2,1,0:T(1,128)S(1)}, u32[]{:S(2)}, u32[]{:S(2)}) collective-permute-start(f32[50,1,128]{2,1,0:T(1,128)S(1)} %get-tuple-element.98), channel_id=1, source_target_pairs={{2,0},{4,2},{6,4},{8,6},{10,8},{12,10},{14,12},{16,14},{18,16},{20... | collective-permute-start | bytes 76808 | tf_op jit(solution)/shard_map/ppermute | solution.py:24
  99.6 0.9 collective-permute-done.17
  101.0 1.1 fusion.226
  102.1 1.4 copy.29
  103.8 1.3 collective-permute-start.19
  105.1 4.7 %collective-permute-start.18 = (f32[50,18,1]{0,1,2:T(8,128)S(1)}, f32[50,18,1]{0,1,2:T(8,128)S(1)}, u32[]{:S(2)}, u32[]{:S(2)}) collective-permute-start(f32[50,18,1]{0,1,2:T(8,128)S(1)} %copy.29), channel_id=1, source_target_pairs={{0,1},{2,3},{4,5},{6,7},{8,9},{10,11},{12,13},{14,15},{16,17},{18,... | collective-permute-start | bytes 10808 | tf_op jit(solution)/shard_map/ppermute | solution.py:22
  109.9 1.1 collective-permute-done.18
  111.4 1.2 copy.32
  112.6 1.8 %fusion.38 = f32[50,16,128]{2,1,0:T(8,128)S(1)} fusion(f32[50,16,128]{2,1,0:T(8,128)S(1)} %fusion.53, f32[50,16,128]{2,1,0:T(8,128)S(1)} %get-tuple-element.42, f32[50,18,1]{2,1,0:T(8,128)} %copy.32, f32[50,1,128]{2,1,0:T(1,128)} %copy-done.26, f32[50,1,128]{2,1,0:T(1,128)} %copy-done.22, f32[50,16,128]{2,1,0:T(8,128)S(1)} %get-tuple-element.41, ...), kind=kLoop, calls=%fused_computation.64 | loop fusion | flops 2969600 | bytes 2559008 | tf_op jit(solution)/shard_map/add | solution.py:74
  114.5 1.9 %collective-permute-start.20 = (f32[50,1,128]{2,1,0:T(1,128)S(1)}, f32[50,1,128]{2,1,0:T(1,128)S(1)}, u32[]{:S(2)}, u32[]{:S(2)}) collective-permute-start(f32[50,1,128]{2,1,0:T(1,128)S(1)} %get-tuple-element.95), channel_id=1, source_target_pairs={{0,2},{2,4},{4,6},{6,8},{8,10},{10,12},{12,14},{14,16},{16,18},{18... | collective-permute-start | bytes 76808 | tf_op jit(solution)/shard_map/ppermute | solution.py:22
  116.4 4.5 %collective-permute-start.21 = (f32[50,1,128]{2,1,0:T(1,128)S(1)}, f32[50,1,128]{2,1,0:T(1,128)S(1)}, u32[]{:S(2)}, u32[]{:S(2)}) collective-permute-start(f32[50,1,128]{2,1,0:T(1,128)S(1)} %get-tuple-element.96), channel_id=1, source_target_pairs={{2,0},{4,2},{6,4},{8,6},{10,8},{12,10},{14,12},{16,14},{18,16},{20... | collective-permute-start | bytes 76808 | tf_op jit(solution)/shard_map/ppermute | solution.py:24
  121.6 0.8 collective-permute-done.21
  123.1 1.1 fusion.225
  124.2 1.4 copy.33
  125.9 1.3 collective-permute-start.23
  127.2 4.5 %collective-permute-start.22 = (f32[50,18,1]{0,1,2:T(8,128)S(1)}, f32[50,18,1]{0,1,2:T(8,128)S(1)}, u32[]{:S(2)}, u32[]{:S(2)}) collective-permute-start(f32[50,18,1]{0,1,2:T(8,128)S(1)} %copy.33), channel_id=1, source_target_pairs={{0,1},{2,3},{4,5},{6,7},{8,9},{10,11},{12,13},{14,15},{16,17},{18,... | collective-permute-start | bytes 10808 | tf_op jit(solution)/shard_map/ppermute | solution.py:22
  131.8 1.3 collective-permute-done.22
  133.5 1.2 copy.36
  134.7 1.8 %fusion.23 = f32[50,16,128]{2,1,0:T(8,128)S(1)} fusion(f32[50,16,128]{2,1,0:T(8,128)S(1)} %fusion.38, f32[50,16,128]{2,1,0:T(8,128)S(1)} %get-tuple-element.42, f32[50,18,1]{2,1,0:T(8,128)} %copy.36, f32[50,1,128]{2,1,0:T(1,128)} %copy-done.24, f32[50,1,128]{2,1,0:T(1,128)} %copy-done.20, f32[50,16,128]{2,1,0:T(8,128)S(1)} %get-tuple-element.41, ...), kind=kLoop, calls=%fused_computation.41 | loop fusion | flops 2969600 | bytes 2559008 | tf_op jit(solution)/shard_map/add | solution.py:74
  136.5 1.9 %collective-permute-start.24 = (f32[50,1,128]{2,1,0:T(1,128)S(1)}, f32[50,1,128]{2,1,0:T(1,128)S(1)}, u32[]{:S(2)}, u32[]{:S(2)}) collective-permute-start(f32[50,1,128]{2,1,0:T(1,128)S(1)} %get-tuple-element.93), channel_id=1, source_target_pairs={{0,2},{2,4},{4,6},{6,8},{8,10},{10,12},{12,14},{14,16},{16,18},{18... | collective-permute-start | bytes 76808 | tf_op jit(solution)/shard_map/ppermute | solution.py:22
  138.5 4.5 %collective-permute-start.25 = (f32[50,1,128]{2,1,0:T(1,128)S(1)}, f32[50,1,128]{2,1,0:T(1,128)S(1)}, u32[]{:S(2)}, u32[]{:S(2)}) collective-permute-start(f32[50,1,128]{2,1,0:T(1,128)S(1)} %get-tuple-element.94), channel_id=1, source_target_pairs={{2,0},{4,2},{6,4},{8,6},{10,8},{12,10},{14,12},{16,14},{18,16},{20... | collective-permute-start | bytes 76808 | tf_op jit(solution)/shard_map/ppermute | solution.py:24
  143.6 0.9 collective-permute-done.25
  145.5 1.3 collective-permute-start.27
  146.8 4.5 %collective-permute-start.26 = (f32[50,18,1]{0,1,2:T(8,128)S(1)}, f32[50,18,1]{0,1,2:T(8,128)S(1)}, u32[]{:S(2)}, u32[]{:S(2)}) collective-permute-start(f32[50,18,1]{0,1,2:T(8,128)S(1)} %copy.37), channel_id=1, source_target_pairs={{0,1},{2,3},{4,5},{6,7},{8,9},{10,11},{12,13},{14,15},{16,17},{18,... | collective-permute-start | bytes 10808 | tf_op jit(solution)/shard_map/ppermute | solution.py:22
  156.4 3.6 %all-to-all-start.2 = ((f32[2,32,128]{2,1,0:T(8,128)}), f32[2,32,128]{2,1,0:T(8,128)S(1)}, u32[]{:S(2)}, u32[]{:S(2)}) async-start(f32[2,32,128]{2,1,0:T(8,128)} %fusion.183), calls=%async_computation.2 | async-start | bytes 65536 | tf_op jit(solution)/shard_map/all_to_all | solution.py:118
  159.9 3.9 %all-to-all-done.2 = f32[2,32,128]{2,1,0:T(8,128)S(1)} async-done(((f32[2,32,128]{2,1,0:T(8,128)}), f32[2,32,128]{2,1,0:T(8,128)S(1)}, u32[]{:S(2)}, u32[]{:S(2)}) %all-to-all-start.2) | async-done | bytes 32800 | tf_op jit(solution)/shard_map/all_to_all | solution.py:118
  163.9 0.9 bitcast_dynamic-update-slice_fusion
  (159 shorter events, 26.0 us)
Async XLA Ops:
  0.6 7.8 %copy-start = (f32[50,16,128]{2,1,0:T(8,128)S(1)}, f32[50,16,128]{2,1,0:T(8,128)}, u32[]{:S(2)}) copy-start(f32[50,16,128]{2,1,0:T(8,128)} %param.17) | copy-start | bytes 1228804
  0.6 12.6 %copy-start.3 = (f32[64,20,128]{2,0,1:T(8,128)S(1)}, f32[64,20,128]{2,0,1:T(8,128)}, u32[]{:S(2)}) copy-start(f32[64,20,128]{2,0,1:T(8,128)} %param.14) | copy-start | bytes 1966084
  5.2 12.8 %all-to-all-start = ((f32[2,1,32]{2,1,0:T(1,128)}), f32[2,1,32]{2,1,0:T(1,128)S(1)}, u32[]{:S(2)}, u32[]{:S(2)}) async-start(f32[2,1,32]{2,1,0:T(1,128)} %bitcast.5), calls=%async_computation | async-start | bytes 2048 | tf_op jit(solution)/shard_map/all_to_all | solution.py:102
  8.4 4.8 %copy-start.16 = (f32[64,128]{1,0:T(8,128)S(1)}, f32[64,128]{1,0:T(8,128)}, u32[]{:S(2)}) copy-start(f32[64,128]{1,0:T(8,128)} %param.15) | copy-start | bytes 98308
  8.5 23.5 %collective-permute-start.2 = (f32[50,1,128]{2,1,0:T(1,128)S(1)}, f32[50,1,128]{2,1,0:T(1,128)S(1)}, u32[]{:S(2)}, u32[]{:S(2)}) collective-permute-start(f32[50,1,128]{2,1,0:T(1,128)S(1)} %get-tuple-element.103), channel_id=1, source_target_pairs={{2,0},{4,2},{6,4},{8,6},{10,8},{12,10},{14,12},{16,14},{18,16},{20... | collective-permute-start | bytes 76808 | tf_op jit(solution)/shard_map/ppermute | solution.py:24
  11.3 20.8 %collective-permute-start = (f32[50,1,128]{2,1,0:T(1,128)S(1)}, f32[50,1,128]{2,1,0:T(1,128)S(1)}, u32[]{:S(2)}, u32[]{:S(2)}) collective-permute-start(f32[50,1,128]{2,1,0:T(1,128)S(1)} %get-tuple-element.104), channel_id=1, source_target_pairs={{0,2},{2,4},{4,6},{6,8},{8,10},{10,12},{12,14},{14,16},{16,18},{18... | collective-permute-start | bytes 76808 | tf_op jit(solution)/shard_map/ppermute | solution.py:22
  14.5 0.6 copy-start.8
  14.5 0.6 copy-start.10
  16.7 0.6 copy-start.4
  16.7 4.7 %copy-start.14 = (f32[64,128]{1,0:T(8,128)}, f32[64,128]{1,0:T(8,128)S(1)}, u32[]{:S(2)}) copy-start(f32[64,128]{1,0:T(8,128)S(1)} %get-tuple-element.35) | copy-start | bytes 98308
  16.8 8.6 %copy-start.1 = (f32[50,16,128]{2,1,0:T(8,128)S(1)}, f32[50,16,128]{2,1,0:T(8,128)}, u32[]{:S(2)}) copy-start(f32[50,16,128]{2,1,0:T(8,128)} %param.16) | copy-start | bytes 1228804
  18.0 7.3 %all-to-all-start.1 = ((f32[2,32,128]{2,1,0:T(8,128)}), f32[2,32,128]{2,1,0:T(8,128)S(1)}, u32[]{:S(2)}, u32[]{:S(2)}) async-start(f32[2,32,128]{2,1,0:T(8,128)} %fusion.106), calls=%async_computation.1 | async-start | bytes 65536 | tf_op jit(solution)/shard_map/all_to_all | solution.py:101
  21.3 10.7 %copy-start.29 = (f32[64,20,128]{2,0,1:T(8,128)}, f32[64,20,128]{2,0,1:T(8,128)S(1)}, u32[]{:S(2)}) copy-start(f32[64,20,128]{2,0,1:T(8,128)S(1)} %constant_dynamic-update-slice_fusion.5) | copy-start | bytes 1966084
  25.5 10.7 %collective-permute-start.1 = (f32[50,1,128]{2,1,0:T(1,128)S(1)}, f32[50,1,128]{2,1,0:T(1,128)S(1)}, u32[]{:S(2)}, u32[]{:S(2)}) collective-permute-start(f32[50,1,128]{2,1,0:T(1,128)S(1)} %get-tuple-element.105), channel_id=1, source_target_pairs={{0,2},{2,4},{4,6},{6,8},{8,10},{10,12},{12,14},{14,16},{16,18},{18... | collective-permute-start | bytes 76808 | tf_op jit(solution)/shard_map/ppermute | solution.py:22
  27.6 8.6 %collective-permute-start.3 = (f32[50,1,128]{2,1,0:T(1,128)S(1)}, f32[50,1,128]{2,1,0:T(1,128)S(1)}, u32[]{:S(2)}, u32[]{:S(2)}) collective-permute-start(f32[50,1,128]{2,1,0:T(1,128)S(1)} %get-tuple-element.106), channel_id=1, source_target_pairs={{2,0},{4,2},{6,4},{8,6},{10,8},{12,10},{14,12},{16,14},{18,16},{20... | collective-permute-start | bytes 76808 | tf_op jit(solution)/shard_map/ppermute | solution.py:24
  33.0 11.0 %collective-permute-start.4 = (f32[50,18,1]{0,1,2:T(8,128)S(1)}, f32[50,18,1]{0,1,2:T(8,128)S(1)}, u32[]{:S(2)}, u32[]{:S(2)}) collective-permute-start(f32[50,18,1]{0,1,2:T(8,128)S(1)} %copy.13), channel_id=1, source_target_pairs={{0,1},{2,3},{4,5},{6,7},{8,9},{10,11},{12,13},{14,15},{16,17},{18,... | collective-permute-start | bytes 10808 | tf_op jit(solution)/shard_map/ppermute | solution.py:22
  34.9 8.7 %collective-permute-start.6 = (f32[50,18,1]{0,1,2:T(8,128)S(1)}, f32[50,18,1]{0,1,2:T(8,128)S(1)}, u32[]{:S(2)}, u32[]{:S(2)}) collective-permute-start(f32[50,18,1]{0,1,2:T(8,128)S(1)} %copy.17), channel_id=1, source_target_pairs={{1,0},{3,2},{5,4},{7,6},{9,8},{11,10},{13,12},{15,14},{17,16},{19,... | collective-permute-start | bytes 10808 | tf_op jit(solution)/shard_map/ppermute | solution.py:24
  36.2 0.6 copy-start.27
  36.2 0.6 copy-start.28
  37.7 8.7 %collective-permute-start.7 = (f32[50,18,1]{0,1,2:T(8,128)S(1)}, f32[50,18,1]{0,1,2:T(8,128)S(1)}, u32[]{:S(2)}, u32[]{:S(2)}) collective-permute-start(f32[50,18,1]{0,1,2:T(8,128)S(1)} %copy.19), channel_id=1, source_target_pairs={{1,0},{3,2},{5,4},{7,6},{9,8},{11,10},{13,12},{15,14},{17,16},{19,... | collective-permute-start | bytes 10808 | tf_op jit(solution)/shard_map/ppermute | solution.py:24
  39.0 6.2 %collective-permute-start.5 = (f32[50,18,1]{0,1,2:T(8,128)S(1)}, f32[50,18,1]{0,1,2:T(8,128)S(1)}, u32[]{:S(2)}, u32[]{:S(2)}) collective-permute-start(f32[50,18,1]{0,1,2:T(8,128)S(1)} %copy.15), channel_id=1, source_target_pairs={{0,1},{2,3},{4,5},{6,7},{8,9},{10,11},{12,13},{14,15},{16,17},{18,... | collective-permute-start | bytes 10808 | tf_op jit(solution)/shard_map/ppermute | solution.py:22
  50.1 6.5 %copy-start.15 = (f32[64,128]{1,0:T(8,128)S(1)}, f32[64,128]{1,0:T(8,128)}, u32[]{:S(2)}) copy-start(f32[64,128]{1,0:T(8,128)} %copy-done.14) | copy-start | bytes 98308
  50.2 7.1 %collective-permute-start.8 = (f32[50,1,128]{2,1,0:T(1,128)S(1)}, f32[50,1,128]{2,1,0:T(1,128)S(1)}, u32[]{:S(2)}, u32[]{:S(2)}) collective-permute-start(f32[50,1,128]{2,1,0:T(1,128)S(1)} %get-tuple-element.101), channel_id=1, source_target_pairs={{0,2},{2,4},{4,6},{6,8},{8,10},{10,12},{12,14},{14,16},{16,18},{18... | collective-permute-start | bytes 76808 | tf_op jit(solution)/shard_map/ppermute | solution.py:22
  52.1 6.1 %collective-permute-start.9 = (f32[50,1,128]{2,1,0:T(1,128)S(1)}, f32[50,1,128]{2,1,0:T(1,128)S(1)}, u32[]{:S(2)}, u32[]{:S(2)}) collective-permute-start(f32[50,1,128]{2,1,0:T(1,128)S(1)} %get-tuple-element.102), channel_id=1, source_target_pairs={{2,0},{4,2},{6,4},{8,6},{10,8},{12,10},{14,12},{16,14},{18,16},{20... | collective-permute-start | bytes 76808 | tf_op jit(solution)/shard_map/ppermute | solution.py:24
  57.3 1.0 copy-start.19
  58.2 0.6 copy-start.23
  61.5 7.6 %collective-permute-start.11 = (f32[50,18,1]{0,1,2:T(8,128)S(1)}, f32[50,18,1]{0,1,2:T(8,128)S(1)}, u32[]{:S(2)}, u32[]{:S(2)}) collective-permute-start(f32[50,18,1]{0,1,2:T(8,128)S(1)} %copy.23), channel_id=1, source_target_pairs={{1,0},{3,2},{5,4},{7,6},{9,8},{11,10},{13,12},{15,14},{17,16},{19,... | collective-permute-start | bytes 10808 | tf_op jit(solution)/shard_map/ppermute | solution.py:24
  62.8 5.9 %collective-permute-start.10 = (f32[50,18,1]{0,1,2:T(8,128)S(1)}, f32[50,18,1]{0,1,2:T(8,128)S(1)}, u32[]{:S(2)}, u32[]{:S(2)}) collective-permute-start(f32[50,18,1]{0,1,2:T(8,128)S(1)} %copy.21), channel_id=1, source_target_pairs={{0,1},{2,3},{4,5},{6,7},{8,9},{10,11},{12,13},{14,15},{16,17},{18,... | collective-permute-start | bytes 10808 | tf_op jit(solution)/shard_map/ppermute | solution.py:22
  72.1 6.6 %copy-start.9 = (f32[64,128]{1,0:T(8,128)S(1)}, f32[64,128]{1,0:T(8,128)}, u32[]{:S(2)}) copy-start(f32[64,128]{1,0:T(8,128)} %copy-done.8) | copy-start | bytes 98308
  72.2 6.6 %copy-start.11 = (f32[64,128]{1,0:T(8,128)S(1)}, f32[64,128]{1,0:T(8,128)}, u32[]{:S(2)}) copy-start(f32[64,128]{1,0:T(8,128)} %copy-done.10) | copy-start | bytes 98308
  72.2 6.6 %copy-start.12 = (f32[64,128]{1,0:T(8,128)S(1)}, f32[64,128]{1,0:T(8,128)}, u32[]{:S(2)}) copy-start(f32[64,128]{1,0:T(8,128)} %get-tuple-element.36) | copy-start | bytes 98308
  72.2 7.1 %collective-permute-start.12 = (f32[50,1,128]{2,1,0:T(1,128)S(1)}, f32[50,1,128]{2,1,0:T(1,128)S(1)}, u32[]{:S(2)}, u32[]{:S(2)}) collective-permute-start(f32[50,1,128]{2,1,0:T(1,128)S(1)} %get-tuple-element.99), channel_id=1, source_target_pairs={{0,2},{2,4},{4,6},{6,8},{8,10},{10,12},{12,14},{14,16},{16,18},{18... | collective-permute-start | bytes 76808 | tf_op jit(solution)/shard_map/ppermute | solution.py:22
  74.1 6.1 %collective-permute-start.13 = (f32[50,1,128]{2,1,0:T(1,128)S(1)}, f32[50,1,128]{2,1,0:T(1,128)S(1)}, u32[]{:S(2)}, u32[]{:S(2)}) collective-permute-start(f32[50,1,128]{2,1,0:T(1,128)S(1)} %get-tuple-element.100), channel_id=1, source_target_pairs={{2,0},{4,2},{6,4},{8,6},{10,8},{12,10},{14,12},{16,14},{18,16},{20... | collective-permute-start | bytes 76808 | tf_op jit(solution)/shard_map/ppermute | solution.py:24
  79.4 0.9 copy-start.21
  80.2 0.6 copy-start.25
  81.8 7.6 %collective-permute-start.15 = (f32[50,18,1]{0,1,2:T(8,128)S(1)}, f32[50,18,1]{0,1,2:T(8,128)S(1)}, u32[]{:S(2)}, u32[]{:S(2)}) collective-permute-start(f32[50,18,1]{0,1,2:T(8,128)S(1)} %copy.27), channel_id=1, source_target_pairs={{1,0},{3,2},{5,4},{7,6},{9,8},{11,10},{13,12},{15,14},{17,16},{19,... | collective-permute-start | bytes 10808 | tf_op jit(solution)/shard_map/ppermute | solution.py:24
  83.1 5.9 %collective-permute-start.14 = (f32[50,18,1]{0,1,2:T(8,128)S(1)}, f32[50,18,1]{0,1,2:T(8,128)S(1)}, u32[]{:S(2)}, u32[]{:S(2)}) collective-permute-start(f32[50,18,1]{0,1,2:T(8,128)S(1)} %copy.25), channel_id=1, source_target_pairs={{0,1},{2,3},{4,5},{6,7},{8,9},{10,11},{12,13},{14,15},{16,17},{18,... | collective-permute-start | bytes 10808 | tf_op jit(solution)/shard_map/ppermute | solution.py:22
  92.4 6.5 %copy-start.13 = (f32[64,128]{1,0:T(8,128)S(1)}, f32[64,128]{1,0:T(8,128)}, u32[]{:S(2)}) copy-start(f32[64,128]{1,0:T(8,128)} %get-tuple-element.36) | copy-start | bytes 98308
  92.4 7.1 %collective-permute-start.16 = (f32[50,1,128]{2,1,0:T(1,128)S(1)}, f32[50,1,128]{2,1,0:T(1,128)S(1)}, u32[]{:S(2)}, u32[]{:S(2)}) collective-permute-start(f32[50,1,128]{2,1,0:T(1,128)S(1)} %get-tuple-element.97), channel_id=1, source_target_pairs={{0,2},{2,4},{4,6},{6,8},{8,10},{10,12},{12,14},{14,16},{16,18},{18... | collective-permute-start | bytes 76808 | tf_op jit(solution)/shard_map/ppermute | solution.py:22
  94.4 6.1 %collective-permute-start.17 = (f32[50,1,128]{2,1,0:T(1,128)S(1)}, f32[50,1,128]{2,1,0:T(1,128)S(1)}, u32[]{:S(2)}, u32[]{:S(2)}) collective-permute-start(f32[50,1,128]{2,1,0:T(1,128)S(1)} %get-tuple-element.98), channel_id=1, source_target_pairs={{2,0},{4,2},{6,4},{8,6},{10,8},{12,10},{14,12},{16,14},{18,16},{20... | collective-permute-start | bytes 76808 | tf_op jit(solution)/shard_map/ppermute | solution.py:24
  99.6 1.0 copy-start.22
  100.4 0.6 copy-start.26
  103.8 7.6 %collective-permute-start.19 = (f32[50,18,1]{0,1,2:T(8,128)S(1)}, f32[50,18,1]{0,1,2:T(8,128)S(1)}, u32[]{:S(2)}, u32[]{:S(2)}) collective-permute-start(f32[50,18,1]{0,1,2:T(8,128)S(1)} %copy.31), channel_id=1, source_target_pairs={{1,0},{3,2},{5,4},{7,6},{9,8},{11,10},{13,12},{15,14},{17,16},{19,... | collective-permute-start | bytes 10808 | tf_op jit(solution)/shard_map/ppermute | solution.py:24
  105.1 5.9 %collective-permute-start.18 = (f32[50,18,1]{0,1,2:T(8,128)S(1)}, f32[50,18,1]{0,1,2:T(8,128)S(1)}, u32[]{:S(2)}, u32[]{:S(2)}) collective-permute-start(f32[50,18,1]{0,1,2:T(8,128)S(1)} %copy.29), channel_id=1, source_target_pairs={{0,1},{2,3},{4,5},{6,7},{8,9},{10,11},{12,13},{14,15},{16,17},{18,... | collective-permute-start | bytes 10808 | tf_op jit(solution)/shard_map/ppermute | solution.py:22
  114.4 6.6 %copy-start.5 = (f32[64,128]{1,0:T(8,128)S(1)}, f32[64,128]{1,0:T(8,128)}, u32[]{:S(2)}) copy-start(f32[64,128]{1,0:T(8,128)} %copy-done.4) | copy-start | bytes 98308
  114.4 6.6 %copy-start.17 = (f32[64,128]{1,0:T(8,128)S(1)}, f32[64,128]{1,0:T(8,128)}, u32[]{:S(2)}) copy-start(f32[64,128]{1,0:T(8,128)} %get-tuple-element.38) | copy-start | bytes 98308
  114.4 6.6 %copy-start.18 = (f32[64,128]{1,0:T(8,128)S(1)}, f32[64,128]{1,0:T(8,128)}, u32[]{:S(2)}) copy-start(f32[64,128]{1,0:T(8,128)} %get-tuple-element.39) | copy-start | bytes 98308
  114.5 7.1 %collective-permute-start.20 = (f32[50,1,128]{2,1,0:T(1,128)S(1)}, f32[50,1,128]{2,1,0:T(1,128)S(1)}, u32[]{:S(2)}, u32[]{:S(2)}) collective-permute-start(f32[50,1,128]{2,1,0:T(1,128)S(1)} %get-tuple-element.95), channel_id=1, source_target_pairs={{0,2},{2,4},{4,6},{6,8},{8,10},{10,12},{12,14},{14,16},{16,18},{18... | collective-permute-start | bytes 76808 | tf_op jit(solution)/shard_map/ppermute | solution.py:22
  116.4 6.1 %collective-permute-start.21 = (f32[50,1,128]{2,1,0:T(1,128)S(1)}, f32[50,1,128]{2,1,0:T(1,128)S(1)}, u32[]{:S(2)}, u32[]{:S(2)}) collective-permute-start(f32[50,1,128]{2,1,0:T(1,128)S(1)} %get-tuple-element.96), channel_id=1, source_target_pairs={{2,0},{4,2},{6,4},{8,6},{10,8},{12,10},{14,12},{16,14},{18,16},{20... | collective-permute-start | bytes 76808 | tf_op jit(solution)/shard_map/ppermute | solution.py:24
  121.6 0.9 copy-start.20
  122.5 0.6 copy-start.24
  125.9 7.6 %collective-permute-start.23 = (f32[50,18,1]{0,1,2:T(8,128)S(1)}, f32[50,18,1]{0,1,2:T(8,128)S(1)}, u32[]{:S(2)}, u32[]{:S(2)}) collective-permute-start(f32[50,18,1]{0,1,2:T(8,128)S(1)} %copy.35), channel_id=1, source_target_pairs={{1,0},{3,2},{5,4},{7,6},{9,8},{11,10},{13,12},{15,14},{17,16},{19,... | collective-permute-start | bytes 10808 | tf_op jit(solution)/shard_map/ppermute | solution.py:24
  127.2 5.9 %collective-permute-start.22 = (f32[50,18,1]{0,1,2:T(8,128)S(1)}, f32[50,18,1]{0,1,2:T(8,128)S(1)}, u32[]{:S(2)}, u32[]{:S(2)}) collective-permute-start(f32[50,18,1]{0,1,2:T(8,128)S(1)} %copy.33), channel_id=1, source_target_pairs={{0,1},{2,3},{4,5},{6,7},{8,9},{10,11},{12,13},{14,15},{16,17},{18,... | collective-permute-start | bytes 10808 | tf_op jit(solution)/shard_map/ppermute | solution.py:22
  136.5 6.5 %copy-start.6 = (f32[64,128]{1,0:T(8,128)S(1)}, f32[64,128]{1,0:T(8,128)}, u32[]{:S(2)}) copy-start(f32[64,128]{1,0:T(8,128)} %copy-done.4) | copy-start | bytes 98308
  136.5 7.1 %collective-permute-start.24 = (f32[50,1,128]{2,1,0:T(1,128)S(1)}, f32[50,1,128]{2,1,0:T(1,128)S(1)}, u32[]{:S(2)}, u32[]{:S(2)}) collective-permute-start(f32[50,1,128]{2,1,0:T(1,128)S(1)} %get-tuple-element.93), channel_id=1, source_target_pairs={{0,2},{2,4},{4,6},{6,8},{8,10},{10,12},{12,14},{14,16},{16,18},{18... | collective-permute-start | bytes 76808 | tf_op jit(solution)/shard_map/ppermute | solution.py:22
  138.5 6.1 %collective-permute-start.25 = (f32[50,1,128]{2,1,0:T(1,128)S(1)}, f32[50,1,128]{2,1,0:T(1,128)S(1)}, u32[]{:S(2)}, u32[]{:S(2)}) collective-permute-start(f32[50,1,128]{2,1,0:T(1,128)S(1)} %get-tuple-element.94), channel_id=1, source_target_pairs={{2,0},{4,2},{6,4},{8,6},{10,8},{12,10},{14,12},{16,14},{18,16},{20... | collective-permute-start | bytes 76808 | tf_op jit(solution)/shard_map/ppermute | solution.py:24
  145.5 7.6 %collective-permute-start.27 = (f32[50,18,1]{0,1,2:T(8,128)S(1)}, f32[50,18,1]{0,1,2:T(8,128)S(1)}, u32[]{:S(2)}, u32[]{:S(2)}) collective-permute-start(f32[50,18,1]{0,1,2:T(8,128)S(1)} %copy.39), channel_id=1, source_target_pairs={{1,0},{3,2},{5,4},{7,6},{9,8},{11,10},{13,12},{15,14},{17,16},{19,... | collective-permute-start | bytes 10808 | tf_op jit(solution)/shard_map/ppermute | solution.py:24
  146.8 5.9 %collective-permute-start.26 = (f32[50,18,1]{0,1,2:T(8,128)S(1)}, f32[50,18,1]{0,1,2:T(8,128)S(1)}, u32[]{:S(2)}, u32[]{:S(2)}) collective-permute-start(f32[50,18,1]{0,1,2:T(8,128)S(1)} %copy.37), channel_id=1, source_target_pairs={{0,1},{2,3},{4,5},{6,7},{8,9},{10,11},{12,13},{14,15},{16,17},{18,... | collective-permute-start | bytes 10808 | tf_op jit(solution)/shard_map/ppermute | solution.py:22
  153.1 1.0 copy-start.2
  154.8 0.8 copy-start.7
  156.4 7.5 %all-to-all-start.2 = ((f32[2,32,128]{2,1,0:T(8,128)}), f32[2,32,128]{2,1,0:T(8,128)S(1)}, u32[]{:S(2)}, u32[]{:S(2)}) async-start(f32[2,32,128]{2,1,0:T(8,128)} %fusion.183), calls=%async_computation.2 | async-start | bytes 65536 | tf_op jit(solution)/shard_map/all_to_all | solution.py:118
  164.7 0.7 copy-start.30
where the time goes:
time: 168 us; the launch traced here: 166 us
  starting transfers between devices  91.8 us (55%)
  local copies, waits for them, and re-layouts  31.1 us (19%)
  other arithmetic  20.2 us (12%)
  waiting for transfers between devices  16.6 us (10%)
  matrix products  4.15 us (2%)
  between operations  2.27 us (1%)
    ppermute x14, starting transfers between devices, with_halo(): lax.ppermute(tail, axis, [(i, (i + 1) % count) for i in range(ends)])  42.9 us
    ppermute x14, starting transfers between devices, with_halo(): lax.ppermute(head, axis, [((i + 1) % count, i) for i in range(ends)])  39 us
    add x6, other arithmetic, lateral_core(): return centre + flow_rate * flux_total  10.6 us
    slice x19, local copies, waits for them, and re-layouts, with_halo(): lax.slice_in_dim(cells, cells.shape[dim] - width, cells.shape[dim], axis=...  9.48 us
    unnamed x71, local copies, waits for them, and re-layouts  7.03 us
    ppermute x7, local copies, waits for them, and re-layouts, with_halo(): lax.ppermute(head, axis, [((i + 1) % count, i) for i in range(ends)])  6.68 us
    ppermute x14, waiting for transfers between devices, with_halo(): lax.ppermute(tail, axis, [(i, (i + 1) % count) for i in range(ends)])  5.65 us
    ppermute x14, waiting for transfers between devices, with_halo(): lax.ppermute(head, axis, [((i + 1) % count, i) for i in range(ends)])  4.33 us
  transfers between devices with their start and end apart: 31, of which 12 were waited for; matrix products, arithmetic and copies ran while one was open for 10% of the time, Pallas kernels for 0%

commit v1 on v0

v1 whole, which is shorter than its diff:
```python
import functools

import jax
import jax.numpy as jnp
from jax import lax
from jax.experimental import pallas as pl
from jax.experimental.pallas import tpu as pltpu
from jax.sharding import PartitionSpec as P

PATCH_DEV = 8
SWEEPS = 6
HALO = 8
SLOT = 2 * HALO
LANES = 128
MESH = pl.DeviceIdType.MESH

flow_rate = 0.15
capillary = 0.5


def one_hot_rows(tile, offset, used_count, tile_count, tile_rows):
    blocks = tile.shape[1]
    block = lax.broadcasted_iota(jnp.int32, (1, blocks), 1)
    target = jnp.where(block < used_count, tile * tile_rows + offset, -1)
    slot = lax.broadcasted_iota(jnp.int32, (tile_count * tile_rows, blocks), 0)
    return (slot == target).astype(jnp.float32)


def flow_kernel(
    sizes,
    moist_in, diff_in, rain_in, head_in, cond_in, tile_ref, offset_ref, count_ref,
    field_out, wet_out, surf_out,
    h, k, w_e, w_s, w_v, delta, packed, land_l, land_r, moist, diff, ratio, rain,
    recharge, surf,
    local_sem, out_sem, row_send, row_recv, pack_send, pack_recv, rech_send, rech_recv,
    surf_send, surf_recv,
):
    rows_n, cols_n, nz, tile_rows = sizes
    gx, gy = lax.axis_index("gx"), lax.axis_index("gy")
    has_below, has_above = gx < rows_n - 1, gx > 0
    has_right, has_left = gy < cols_n - 1, gy > 0
    depth = moist.shape[0]
    groups = packed.shape[1]
    ring_rows, ring_cols = h.shape[1], h.shape[2]
    below = pl.ds(tile_rows, HALO)
    above = pl.ds(tile_rows + HALO, HALO)
    first = pl.ds(0, HALO)
    last = pl.ds(tile_rows - HALO, HALO)
    whole = pl.ds(0, tile_rows)
    main = pl.ds(0, LANES)

    local = [
        pltpu.make_async_copy(src, dst, local_sem.at[i])
        for i, (src, dst) in enumerate((
            (head_in, h.at[pl.ds(0, nz), whole, main]),
            (cond_in, k.at[pl.ds(0, nz), whole, main]),
            (moist_in, moist),
            (diff_in, diff),
            (rain_in, rain),
        ))
    ]
    for copy in local:
        copy.start()

    row_steps = ((0, None, whole, whole), (1, has_below, above, last), (-1, has_above, below, first))
    peers = []
    for dx, exists, _, _ in row_steps:
        for dy in range(cols_n):
            if dx or dy:
                peers.append((dx, exists, lax.rem(gy + dy, cols_n)))

    def when(cond, body):
        if cond is None:
            body()
        else:
            pl.when(cond)(body)

    def both(a, b):
        return b if a is None else jnp.logical_and(a, b)

    barrier = pltpu.get_barrier_semaphore()
    for dx, exists, col in peers:
        def greet(dx=dx, col=col):
            pl.semaphore_signal(barrier, inc=1, device_id=(gx + dx, col), device_id_type=MESH)
        when(exists, greet)
    near_rows = 1 + has_below.astype(jnp.int32) + has_above.astype(jnp.int32)
    pl.semaphore_wait(barrier, cols_n * near_rows - 1)

    row_copies = []
    for i, (dx, exists, ring, mine) in enumerate(row_steps[1:]):
        source_exists = has_above if dx == 1 else has_below
        for f, (src, dst) in enumerate(((head_in, h), (cond_in, k))):
            row_copies.append((exists, source_exists, pltpu.make_async_remote_copy(
                src_ref=src.at[:, mine],
                dst_ref=dst.at[pl.ds(0, nz), ring, main],
                send_sem=row_send.at[2 * i + f],
                recv_sem=row_recv.at[2 * i + f],
                device_id=(gx + dx, gy),
                device_id_type=MESH,
            )))
    for exists, _, copy in row_copies:
        when(exists, copy.start)

    local[0].wait()
    local[1].wait()
    lane = lax.broadcasted_iota(jnp.int32, (1, LANES), 1)

    def zero_tail(z, _):
        h[z] = jnp.zeros((ring_rows, ring_cols), jnp.float32)
        k[z] = jnp.zeros((ring_rows, ring_cols), jnp.float32)
        return 0
    lax.fori_loop(nz, h.shape[0], zero_tail, 0)

    def pack(g, _):
        for f, src in enumerate((h, k)):
            total = jnp.zeros((tile_rows, LANES), jnp.float32)
            for s in range(LANES // SLOT):
                edge = pltpu.roll(src[g * (LANES // SLOT) + s, 0:tile_rows, 0:LANES], (HALO + SLOT * s) % LANES, 1)
                inside = (lane >= SLOT * s) & (lane < SLOT * (s + 1))
                total = jnp.where(inside, edge, total)
            packed[f, g] = total
        return 0
    lax.fori_loop(0, groups, pack, 0)

    pack_copies = []
    n = 0
    for dx, exists, ring, mine in row_steps:
        source_row = None if dx == 0 else (has_above if dx == 1 else has_below)
        for dy, side, target, source in ((1, land_l, has_right, has_left), (-1, land_r, has_left, has_right)):
            pack_copies.append((both(exists, target), both(source_row, source), pltpu.make_async_remote_copy(
                src_ref=packed.at[:, :, mine],
                dst_ref=side.at[:, :, ring],
                send_sem=pack_send.at[n],
                recv_sem=pack_recv.at[n],
                device_id=(gx + dx, gy + dy),
                device_id_type=MESH,
            )))
            n += 1
    for exists, _, copy in pack_copies:
        when(exists, copy.start)

    for copy in local[2:]:
        copy.wait()
    e0 = diff[0]
    inv = 1.0 / (1.0 + e0)
    r0, f0 = e0 * inv, (moist[0] + rain[...]) * inv
    ratio[0] = r0
    moist[0] = f0

    def eliminate(layer, carry):
        upper, r, f = carry
        lower = diff[layer]
        inv = 1.0 / (1.0 + lower + upper - upper * r)
        r, f = lower * inv, (moist[layer] + upper * f) * inv
        ratio[layer] = r
        moist[layer] = f
        return lower, r, f
    lower, _, bottom = lax.fori_loop(1, depth, eliminate, (e0, r0, f0))
    drain = lower * bottom
    hot = one_hot_rows(tile_ref[...], offset_ref[...], count_ref[0], cols_n, tile_rows)
    mine = jnp.dot(hot, drain, precision=lax.Precision.HIGHEST, preferred_element_type=jnp.float32)
    recharge[0, gy] = mine.reshape(cols_n, tile_rows, LANES)

    rech_copies = []
    n = 0
    for i, (dx, exists, _, rows) in enumerate(row_steps):
        source_row = None if dx == 0 else (has_above if dx == 1 else has_below)
        for dy in range(0 if dx else 1, cols_n):
            to = lax.rem(gy + dy, cols_n)
            came = lax.rem(gy + cols_n - dy, cols_n)
            def copy(slot, to=to, dx=dx, i=i, rows=rows, n=n):
                return pltpu.make_async_remote_copy(
                    src_ref=recharge.at[0, gy, :, rows],
                    dst_ref=recharge.at[i, slot, :, rows],
                    send_sem=rech_send.at[n],
                    recv_sem=rech_recv.at[n],
                    device_id=(gx + dx, to),
                    device_id_type=MESH,
                )
            rech_copies.append((exists, source_row, copy(gy), copy(came)))
            n += 1
    for exists, _, out, _ in rech_copies:
        when(exists, out.start)

    def substitute(i, wet):
        layer = depth - 2 - i
        wet = moist[layer] + ratio[layer] * wet
        moist[layer] = wet
        return wet
    lax.fori_loop(0, depth - 1, substitute, bottom)
    wet_copy = pltpu.make_async_copy(moist, wet_out, out_sem.at[0])
    wet_copy.start()

    ring_row = lax.broadcasted_iota(jnp.int32, (ring_rows, ring_cols), 0)
    ring_col = lax.broadcasted_iota(jnp.int32, (ring_rows, ring_cols), 1)
    row_ok = (ring_row < tile_rows) | ((ring_row < tile_rows + HALO) & has_below) | ((ring_row >= tile_rows + HALO) & has_above)
    col_ok = (ring_col < LANES) | ((ring_col < LANES + LANES // 2) & has_right) | ((ring_col >= LANES + LANES // 2) & has_left)
    mask = (row_ok & col_ok).astype(jnp.float32)
    on_grid = mask > 0.0

    for _, source, copy in row_copies + pack_copies:
        when(source, copy.wait_recv)

    def unpack(g, _):
        for f, dst in enumerate((h, k)):
            comb = jnp.where((lane % SLOT) < HALO, land_l[f, g], land_r[f, g])
            for s in range(LANES // SLOT):
                z = g * (LANES // SLOT) + s
                side = pltpu.roll(comb, (LANES - HALO - SLOT * s) % LANES, 1)
                full = jnp.concatenate([dst[z, :, 0:LANES], side], axis=1)
                dst[z] = jnp.where(on_grid, full, 0.0)
        return 0
    lax.fori_loop(0, groups, unpack, 0)

    scale = 0.5 * flow_rate

    def weights(z, here):
        after = k[z + 1]
        w_e[z] = scale * (here + pltpu.roll(here, ring_cols - 1, 1))
        w_s[z] = scale * (here + pltpu.roll(here, ring_rows - 1, 0))
        w_v[z] = jnp.where(z < nz - 1, scale, 0.0) * (here + after)
        return after
    lax.fori_loop(0, nz, weights, k[0])

    def step(cells, z, carry, last):
        here, f_up = carry
        f_e = w_e[z] * (pltpu.roll(here, ring_cols - 1, 1) - here)
        f_s = w_s[z] * (pltpu.roll(here, ring_rows - 1, 0) - here)
        if last:
            after, f_v = here, jnp.zeros_like(here)
        else:
            after = cells[z + 1]
            f_v = w_v[z] * (after - here)
        change = (f_e - pltpu.roll(f_e, 1, 1)) + (f_s - pltpu.roll(f_s, 1, 0)) + (f_v - f_up)
        cells[z] = here + mask * change
        return after, f_v

    zeros = jnp.zeros((ring_rows, ring_cols), jnp.float32)

    def base_sweep(_, c):
        carry = lax.fori_loop(0, nz - 1, lambda z, carry: step(h, z, carry, False), (h[0], zeros))
        step(h, nz - 1, carry, True)
        return c
    lax.fori_loop(0, SWEEPS, base_sweep, 0)

    for _, source, _, arrived in rech_copies:
        when(source, arrived.wait_recv)

    def tile_sum(tile):
        parts = []
        for i, rows in ((0, whole), (1, last), (2, first)):
            total = recharge[i, 0, tile, rows]
            for s in range(1, cols_n):
                total = total + recharge[i, s, tile, rows]
            parts.append(total)
        return jnp.concatenate([parts[0], parts[2], parts[1]], axis=0)
    centre = tile_sum(gy)
    right = tile_sum(jnp.minimum(gy + 1, cols_n - 1))
    left = tile_sum(jnp.maximum(gy - 1, 0))
    side = jnp.where(lane < LANES // 2, right, left)
    delta[0] = jnp.where(on_grid, jnp.concatenate([centre, side], axis=1), 0.0)
    for z in range(1, SWEEPS + 2):
        delta[z] = zeros
    for sweep in range(SWEEPS):
        reach = min(sweep + 2, nz)
        lax.fori_loop(0, reach, lambda z, carry: step(delta, z, carry, False), (delta[0], zeros))
    for z in range(min(SWEEPS + 1, nz)):
        h[z, 0:tile_rows, 0:LANES] = h[z, 0:tile_rows, 0:LANES] + delta[z, 0:tile_rows, 0:LANES]

    surf[gy] = h[0, 0:tile_rows, 0:LANES]
    surf_copies = []
    for dy in range(1, cols_n):
        to = lax.rem(gy + dy, cols_n)
        came = lax.rem(gy + cols_n - dy, cols_n)
        pair = [
            pltpu.make_async_remote_copy(
                src_ref=surf.at[gy],
                dst_ref=surf.at[slot],
                send_sem=surf_send.at[dy - 1],
                recv_sem=surf_recv.at[dy - 1],
                device_id=(gx, to),
                device_id_type=MESH,
            )
            for slot in (gy, came)
        ]
        pair[0].start()
        surf_copies.append(pair)
    field_copy = pltpu.make_async_copy(h.at[pl.ds(0, nz), whole, main], field_out, out_sem.at[1])
    field_copy.start()
    for _, arrived in surf_copies:
        arrived.wait_recv()
    surf_copy = pltpu.make_async_copy(surf, surf_out, out_sem.at[2])
    surf_copy.start()

    for exists, _, copy in row_copies + pack_copies:
        when(exists, copy.wait_send)
    for exists, _, out, _ in rech_copies:
        when(exists, out.wait_send)
    for out, _ in surf_copies:
        out.wait_send()
    wet_copy.wait()
    field_copy.wait()
    surf_copy.wait()


def exchange_kernel(
    tile_rows, cols_n,
    field, wet, surf, tile_ref, offset_ref, patch_ref, count_ref,
    head_out, moist_out, patch_out,
    bottom, sem,
):
    depth, blocks, _ = wet.shape
    load = pltpu.make_async_copy(wet.at[depth - 1], bottom, sem.at[0])
    load.start()
    copies = [
        pltpu.make_async_copy(wet.at[pl.ds(0, depth - 1)], moist_out.at[pl.ds(0, depth - 1)], sem.at[1]),
        pltpu.make_async_copy(field, head_out, sem.at[2]),
    ]
    for copy in copies:
        copy.start()
    hot = one_hot_rows(tile_ref[...], offset_ref[...], count_ref[0], cols_n, tile_rows)
    surface = surf[...].reshape(cols_n * tile_rows, LANES)
    saturation = lax.dot_general(
        hot, surface, (((0,), (0,)), ((), ())),
        precision=lax.Precision.HIGHEST, preferred_element_type=jnp.float32,
    )
    patch = lax.broadcasted_iota(jnp.int32, (PATCH_DEV, blocks), 0)
    patch_hot = (patch == patch_ref[...]).astype(jnp.float32)
    patch_out[...] = jnp.dot(
        patch_hot, saturation, precision=lax.Precision.HIGHEST, preferred_element_type=jnp.float32
    )
    used = (lax.broadcasted_iota(jnp.int32, (blocks, LANES), 0) < count_ref[0]).astype(jnp.float32)
    load.wait()
    wet_bottom = bottom[...]
    bottom[...] = wet_bottom + capillary * (saturation - used * wet_bottom)
    store = pltpu.make_async_copy(bottom, moist_out.at[depth - 1], sem.at[0])
    store.start()
    store.wait()
    for copy in copies:
        copy.wait()


def local(rows_n, cols_n, moisture, diffusivity, rain, head, conductivity, tile_ids, offsets, patch_ids, counts):
    blocks, depth, _ = moisture.shape
    nz, tile_rows, _ = head.shape
    moisture = jnp.transpose(moisture, (1, 0, 2))
    diffusivity = jnp.transpose(diffusivity, (1, 0, 2))
    tile_ids, offsets, patch_ids = (x.reshape(1, blocks) for x in (tile_ids, offsets, patch_ids))
    f32 = jnp.float32
    per = LANES // SLOT
    groups = pl.cdiv(nz, per)
    ring = (tile_rows + 2 * HALO, 2 * LANES)
    hbm = pl.BlockSpec(memory_space=pl.ANY)
    vmem = pl.BlockSpec(memory_space=pltpu.VMEM)
    smem = pl.BlockSpec(memory_space=pltpu.SMEM)
    dma = pltpu.SemaphoreType.DMA
    rech = 3 * cols_n - 1
    field, wet, surf = pl.pallas_call(
        functools.partial(flow_kernel, (rows_n, cols_n, nz, tile_rows)),
        name="flow",
        out_shape=(
            jax.ShapeDtypeStruct((nz, tile_rows, LANES), f32),
            jax.ShapeDtypeStruct((depth, blocks, LANES), f32),
            jax.ShapeDtypeStruct((cols_n, tile_rows, LANES), f32),
        ),
        in_specs=[hbm] * 5 + [vmem] * 2 + [smem],
        out_specs=(hbm,) * 3,
        scratch_shapes=[
            pltpu.VMEM((groups * per,) + ring, f32),
            pltpu.VMEM((groups * per,) + ring, f32),
            pltpu.VMEM((nz,) + ring, f32),
            pltpu.VMEM((nz,) + ring, f32),
            pltpu.VMEM((nz,) + ring, f32),
            pltpu.VMEM((SWEEPS + 2,) + ring, f32),
            pltpu.VMEM((2, groups, tile_rows, LANES), f32),
            pltpu.VMEM((2, groups, ring[0], LANES), f32),
            pltpu.VMEM((2, groups, ring[0], LANES), f32),
            pltpu.VMEM((depth, blocks, LANES), f32),
            pltpu.VMEM((depth, blocks, LANES), f32),
            pltpu.VMEM((depth, blocks, LANES), f32),
            pltpu.VMEM((blocks, LANES), f32),
            pltpu.VMEM((3, cols_n, cols_n, tile_rows, LANES), f32),
            pltpu.VMEM((cols_n, tile_rows, LANES), f32),
            dma((5,)), dma((3,)), dma((4,)), dma((4,)), dma((6,)), dma((6,)),
            dma((rech,)), dma((rech,)), dma((cols_n,)), dma((cols_n,)),
        ],
        compiler_params=pltpu.CompilerParams(
            collective_id=0, has_side_effects=True, vmem_limit_bytes=32 * 1024 * 1024
        ),
    )(moisture, diffusivity, rain, head, conductivity, tile_ids, offsets, counts)
    head_out, moist_out, patch_sums = pl.pallas_call(
        functools.partial(exchange_kernel, tile_rows, cols_n),
        name="exchange",
        out_shape=(
            jax.ShapeDtypeStruct((nz, tile_rows, LANES), f32),
            jax.ShapeDtypeStruct((depth, blocks, LANES), f32),
            jax.ShapeDtypeStruct((PATCH_DEV, LANES), f32),
        ),
        in_specs=[hbm, hbm] + [vmem] * 4 + [smem],
        out_specs=(hbm, hbm, vmem),
        scratch_shapes=[pltpu.VMEM((blocks, LANES), f32), dma((3,))],
    )(field, wet, surf, tile_ids, offsets, patch_ids, counts)
    return head_out, jnp.transpose(moist_out, (1, 0, 2)), patch_sums


def solution(mesh):
    placed = (
        P(("gx", "gy"), None, None),
        P(("gx", "gy"), None, None),
        P(("gx", "gy"), None),
        P(None, "gx", "gy"),
        P(None, "gx", "gy"),
        P(("gx", "gy")),
        P(("gx", "gy")),
        P(("gx", "gy")),
        P(("gx", "gy")),
    )
    return jax.shard_map(
        functools.partial(local, mesh.shape["gx"], mesh.shape["gy"]),
        mesh=mesh,
        in_specs=placed,
        out_specs=(P(None, "gx", "gy"), P(("gx", "gy"), None, None), P(("gx", "gy"), None)),
        check_vma=False,
    )
```

time: 168 us -> 116 us (0.69)
  the two profiles are of different devices: /device:TPU:24 before, /device:TPU:9 now
where the time goes in v1:
time: 116 us
  Pallas kernels  106 us (91%)
  local copies, waits for them, and re-layouts  7.78 us (7%)
  between operations  1.32 us (1%)
    pallas_call x1, Pallas kernels, local(): pl.pallas_call(functools.partial(flow_kernel, (rows_n, cols_n, nz, tile_r...  72.7 us
    pallas_call x1, Pallas kernels, local(): pl.pallas_call(functools.partial(exchange_kernel, tile_rows, cols_n), nam...  33.7 us
    unnamed x20, local copies, waits for them, and re-layouts  7.78 us

profile of v1, /device:TPU:9, one launch (start us, length us, event | category | flops | bytes accessed | tf_op | source)
XLA Modules:
  0.0 115.5 jit_solution(13408030710086266553)
XLA Ops:
  1.3 0.0 copy-start.8
  1.3 0.0 copy-start.9
  1.3 0.6 copy-done.8
  1.9 0.0 copy-done.9
  2.0 0.0 copy-start
  2.0 1.1 copy-done
  3.0 0.0 copy-start.1
  3.0 1.1 copy-done.1
  4.1 0.0 copy-start.4
  4.1 1.0 copy-done.4
  5.1 0.0 copy-start.5
  5.1 1.0 copy-done.5
  6.1 0.0 copy-start.6
  6.1 0.8 copy-done.6
  6.9 72.7 %flow.1 = (f32[50,16,128]{2,1,0:T(8,128)S(1)}, f32[20,64,128]{2,1,0:T(8,128)S(1)}, f32[2,16,128]{2,1,0:T(8,128)S(1)}) custom-call(f32[20,64,128]{2,1,0:T(8,128)S(1)} %bitcast.6, f32[20,64,128]{2,1,0:T(8,128)S(1)} %bitcast.7, f32[64,128]{1,0:T(8,128)S(1)} %copy-done.6, f32[50,16,128]{2,1,0:T(8,128)S(1)} %copy-done.4, f32[50,16,128]{2,1,0:T(8,128)S(1)} %copy-done.5, ...), custom_call_target="tpu_custom_call" | custom-call | tf_op jit(solution)/shard_map/flow/pallas_call | solution.py:358
  79.6 0.0 copy-start.2
  79.6 0.8 copy-done.2
  80.4 0.0 copy-start.3
  80.4 0.8 copy-done.3
  81.2 0.0 copy-start.7
  81.2 0.6 copy-done.7
  81.8 33.7 %exchange.1 = (f32[50,16,128]{2,1,0:T(8,128)}, f32[20,64,128]{2,1,0:T(8,128)}, f32[8,128]{1,0:T(8,128)}) custom-call(f32[50,16,128]{2,1,0:T(8,128)} %copy-done.3, f32[20,64,128]{2,1,0:T(8,128)} %copy-done.2, f32[2,16,128]{2,1,0:T(8,128)} %copy-done.7, s32[1,64]{1,0:T(1,128)} %bitcast.8, s32[1,64]{1,0:T(1,128)} %bitcast.10, s32[1,64]{1,0:T(1,128)} %bitcast.12, ...), custom_call_target="tpu_custom_call" | custom-call | tf_op jit(solution)/shard_map/exchange/pallas_call | solution.py:391
Async XLA Ops:
  1.3 0.7 copy-start.8
  1.3 0.7 copy-start.9
  2.0 1.1 copy-start
  3.0 1.1 copy-start.1
  4.1 1.0 copy-start.4
  5.1 1.0 copy-start.5
  6.1 0.8 copy-start.6
  79.6 0.8 copy-start.2
  80.4 0.8 copy-start.3
  81.2 0.6 copy-start.7

commit v2 on v1

--- a/solution.py
+++ b/solution.py
@@ -28,10 +28,10 @@
 
 def flow_kernel(
     sizes,
-    moist_in, diff_in, rain_in, head_in, cond_in, tile_ref, offset_ref, count_ref,
+    moist_in, diff_in, rain_in, head_in, cond_in, tile_in, offset_in, count_ref,
     field_out, wet_out, surf_out,
     h, k, w_e, w_s, w_v, delta, packed, land_l, land_r, moist, diff, ratio, rain,
-    recharge, surf,
+    tile_ref, offset_ref, recharge, surf,
     local_sem, out_sem, row_send, row_recv, pack_send, pack_recv, rech_send, rech_recv,
     surf_send, surf_recv,
 ):
@@ -57,6 +57,8 @@
             (moist_in, moist),
             (diff_in, diff),
             (rain_in, rain),
+            (tile_in, tile_ref),
+            (offset_in, offset_ref),
         ))
     ]
     for copy in local:
@@ -305,19 +307,28 @@
 
 def exchange_kernel(
     tile_rows, cols_n,
-    field, wet, surf, tile_ref, offset_ref, patch_ref, count_ref,
+    field_in, wet_in, surf_in, tile_in, offset_in, patch_in, count_ref,
     head_out, moist_out, patch_out,
-    bottom, sem,
+    field, wet, surf, tile_ref, offset_ref, patch_ref, sem,
 ):
     depth, blocks, _ = wet.shape
-    load = pltpu.make_async_copy(wet.at[depth - 1], bottom, sem.at[0])
-    load.start()
-    copies = [
-        pltpu.make_async_copy(wet.at[pl.ds(0, depth - 1)], moist_out.at[pl.ds(0, depth - 1)], sem.at[1]),
-        pltpu.make_async_copy(field, head_out, sem.at[2]),
+    upper = pl.ds(0, depth - 1)
+    loads = [
+        pltpu.make_async_copy(src, dst, sem.at[i])
+        for i, (src, dst) in enumerate((
+            (tile_in, tile_ref),
+            (offset_in, offset_ref),
+            (patch_in, patch_ref),
+            (surf_in, surf),
+            (wet_in.at[depth - 1], wet.at[depth - 1]),
+            (wet_in.at[upper], wet.at[upper]),
+            (field_in, field),
+        ))
     ]
-    for copy in copies:
+    for copy in loads:
         copy.start()
+    for copy in loads[:5]:
+        copy.wait()
     hot = one_hot_rows(tile_ref[...], offset_ref[...], count_ref[0], cols_n, tile_rows)
     surface = surf[...].reshape(cols_n * tile_rows, LANES)
     saturation = lax.dot_general(
@@ -330,14 +341,19 @@
         patch_hot, saturation, precision=lax.Precision.HIGHEST, preferred_element_type=jnp.float32
     )
     used = (lax.broadcasted_iota(jnp.int32, (blocks, LANES), 0) < count_ref[0]).astype(jnp.float32)
-    load.wait()
-    wet_bottom = bottom[...]
-    bottom[...] = wet_bottom + capillary * (saturation - used * wet_bottom)
-    store = pltpu.make_async_copy(bottom, moist_out.at[depth - 1], sem.at[0])
-    store.start()
-    store.wait()
-    for copy in copies:
-        copy.wait()
+    wet_bottom = wet[depth - 1]
+    wet[depth - 1] = wet_bottom + capillary * (saturation - used * wet_bottom)
+    stores = [
+        pltpu.make_async_copy(wet.at[depth - 1], moist_out.at[depth - 1], sem.at[0]),
+        pltpu.make_async_copy(wet.at[upper], moist_out.at[upper], sem.at[1]),
+        pltpu.make_async_copy(field, head_out, sem.at[2]),
+    ]
+    stores[0].start()
+    for load, store in zip(loads[5:], stores[1:]):
+        load.wait()
+        store.start()
+    for store in stores:
+        store.wait()
 
 
 def local(rows_n, cols_n, moisture, diffusivity, rain, head, conductivity, tile_ids, offsets, patch_ids, counts):
@@ -350,7 +366,7 @@
     per = LANES // SLOT
     groups = pl.cdiv(nz, per)
     ring = (tile_rows + 2 * HALO, 2 * LANES)
-    hbm = pl.BlockSpec(memory_space=pl.ANY)
+    hbm = pl.BlockSpec(memory_space=pltpu.HBM)
     vmem = pl.BlockSpec(memory_space=pltpu.VMEM)
     smem = pl.BlockSpec(memory_space=pltpu.SMEM)
     dma = pltpu.SemaphoreType.DMA
@@ -363,7 +379,7 @@
             jax.ShapeDtypeStruct((depth, blocks, LANES), f32),
             jax.ShapeDtypeStruct((cols_n, tile_rows, LANES), f32),
         ),
-        in_specs=[hbm] * 5 + [vmem] * 2 + [smem],
+        in_specs=[hbm] * 7 + [smem],
         out_specs=(hbm,) * 3,
         scratch_shapes=[
             pltpu.VMEM((groups * per,) + ring, f32),
@@ -379,13 +395,15 @@
             pltpu.VMEM((depth, blocks, LANES), f32),
             pltpu.VMEM((depth, blocks, LANES), f32),
             pltpu.VMEM((blocks, LANES), f32),
+            pltpu.VMEM((1, blocks), jnp.int32),
+            pltpu.VMEM((1, blocks), jnp.int32),
             pltpu.VMEM((3, cols_n, cols_n, tile_rows, LANES), f32),
             pltpu.VMEM((cols_n, tile_rows, LANES), f32),
-            dma((5,)), dma((3,)), dma((4,)), dma((4,)), dma((6,)), dma((6,)),
+            dma((7,)), dma((3,)), dma((4,)), dma((4,)), dma((6,)), dma((6,)),
             dma((rech,)), dma((rech,)), dma((cols_n,)), dma((cols_n,)),
         ],
         compiler_params=pltpu.CompilerParams(
-            collective_id=0, has_side_effects=True, vmem_limit_bytes=32 * 1024 * 1024
+            collective_id=0, has_side_effects=True, vmem_limit_bytes=63 * 1024 * 1024
         ),
     )(moisture, diffusivity, rain, head, conductivity, tile_ids, offsets, counts)
     head_out, moist_out, patch_sums = pl.pallas_call(
@@ -396,9 +414,18 @@
             jax.ShapeDtypeStruct((depth, blocks, LANES), f32),
             jax.ShapeDtypeStruct((PATCH_DEV, LANES), f32),
         ),
-        in_specs=[hbm, hbm] + [vmem] * 4 + [smem],
+        in_specs=[hbm] * 6 + [smem],
         out_specs=(hbm, hbm, vmem),
-        scratch_shapes=[pltpu.VMEM((blocks, LANES), f32), dma((3,))],
+        scratch_shapes=[
+            pltpu.VMEM((nz, tile_rows, LANES), f32),
+            pltpu.VMEM((depth, blocks, LANES), f32),
+            pltpu.VMEM((cols_n, tile_rows, LANES), f32),
+            pltpu.VMEM((1, blocks), jnp.int32),
+            pltpu.VMEM((1, blocks), jnp.int32),
+            pltpu.VMEM((1, blocks), jnp.int32),
+            dma((7,)),
+        ],
+        compiler_params=pltpu.CompilerParams(vmem_limit_bytes=63 * 1024 * 1024),
     )(field, wet, surf, tile_ids, offsets, patch_ids, counts)
     return head_out, jnp.transpose(moist_out, (1, 0, 2)), patch_sums
 

time: 116 us -> 77.6 us (0.67)
  Pallas kernels: 106 us -> 75.9 us
  local copies, waits for them, and re-layouts: 7.78 us -> 0 us
    pallas_call x1, Pallas kernels: 33.7 us -> 2.84 us  [local(): pl.pallas_call(functools.partial(exchange_kernel, tile_rows, cols_n), nam...]
    unnamed x20 -> x0, local copies, waits for them, and re-layouts: 7.78 us -> none
where the time goes in v2:
time: 77.6 us; the launch traced here: 77.1 us
  Pallas kernels  75.9 us (98%)
  between operations  1.29 us (2%)
    pallas_call x1, Pallas kernels, local(): pl.pallas_call(functools.partial(flow_kernel, (rows_n, cols_n, nz, tile_r...  73 us
    pallas_call x1, Pallas kernels, local(): pl.pallas_call(functools.partial(exchange_kernel, tile_rows, cols_n), nam...  2.84 us

profile of v2, /device:TPU:9, one launch (start us, length us, event | category | flops | bytes accessed | tf_op | source)
XLA Modules:
  0.0 77.1 jit_solution(7746484034839010869)
XLA Ops:
  1.3 73.0 %flow.1 = (f32[50,16,128]{2,1,0:T(8,128)}, f32[20,64,128]{2,1,0:T(8,128)}, f32[2,16,128]{2,1,0:T(8,128)}) custom-call(f32[20,64,128]{2,1,0:T(8,128)} %bitcast.6, f32[20,64,128]{2,1,0:T(8,128)} %bitcast.7, f32[64,128]{1,0:T(8,128)} %rain_in.1, f32[50,16,128]{2,1,0:T(8,128)} %head_in.1, f32[50,16,128]{2,1,0:T(8,128)} %cond_in.1, s32[1,64]{1,0:T(1,128)} %bitcast.8, ...), custom_call_target="tpu_custom_call" | custom-call | tf_op jit(solution)/shard_map/flow/pallas_call | solution.py:374
  74.3 2.8 %exchange.1 = (f32[50,16,128]{2,1,0:T(8,128)}, f32[20,64,128]{2,1,0:T(8,128)}, f32[8,128]{1,0:T(8,128)}) custom-call(f32[50,16,128]{2,1,0:T(8,128)} %get-tuple-element.9.field_in, f32[20,64,128]{2,1,0:T(8,128)} %get-tuple-element.10.wet_in, f32[2,16,128]{2,1,0:T(8,128)} %get-tuple-element.11.surf_in, s32[1,64]{1,0:T(1,128)} %bitcast.9, s32[1,64]{1,0:T(1,128)} %bitcast.11, ...), custom_call_target="tpu_custom_call" | custom-call | tf_op jit(solution)/shard_map/exchange/pallas_call | solution.py:409

commit v3 on v2

--- a/solution.py
+++ b/solution.py
@@ -10,6 +10,7 @@
 PATCH_DEV = 8
 SWEEPS = 6
 HALO = 8
+BLOCK = 5
 SLOT = 2 * HALO
 LANES = 128
 MESH = pl.DeviceIdType.MESH
@@ -30,7 +31,7 @@
     sizes,
     moist_in, diff_in, rain_in, head_in, cond_in, tile_in, offset_in, count_ref,
     field_out, wet_out, surf_out,
-    h, k, w_e, w_s, w_v, delta, packed, land_l, land_r, moist, diff, ratio, rain,
+    h, h2, k, field, w_d, w_e, w_w, w_s, w_n, w_v, delta, delta2, packed, land_l, land_r, moist, diff, ratio, rain,
     tile_ref, offset_ref, recharge, surf,
     local_sem, out_sem, row_send, row_recv, pack_send, pack_recv, rech_send, rech_recv,
     surf_send, surf_recv,
@@ -48,12 +49,13 @@
     last = pl.ds(tile_rows - HALO, HALO)
     whole = pl.ds(0, tile_rows)
     main = pl.ds(0, LANES)
+    layers = pl.ds(1, nz)
 
     local = [
         pltpu.make_async_copy(src, dst, local_sem.at[i])
         for i, (src, dst) in enumerate((
-            (head_in, h.at[pl.ds(0, nz), whole, main]),
-            (cond_in, k.at[pl.ds(0, nz), whole, main]),
+            (head_in, h.at[layers, whole, main]),
+            (cond_in, k.at[layers, whole, main]),
             (moist_in, moist),
             (diff_in, diff),
             (rain_in, rain),
@@ -80,6 +82,20 @@
     def both(a, b):
         return b if a is None else jnp.logical_and(a, b)
 
+    empty = jnp.zeros((ring_rows, ring_cols), jnp.float32)
+    for ref in (h, h2, k):
+        ref[0] = empty
+        ref[nz + 1] = empty
+
+    def clear(rows):
+        def body(z, _):
+            for ref in (h, k):
+                ref[z, rows, main] = jnp.zeros((HALO, LANES), jnp.float32)
+            return 0
+        lax.fori_loop(1, nz + 1, body, 0)
+    pl.when(gx == 0)(lambda: clear(above))
+    pl.when(gx == rows_n - 1)(lambda: clear(below))
+
     barrier = pltpu.get_barrier_semaphore()
     for dx, exists, col in peers:
         def greet(dx=dx, col=col):
@@ -94,7 +110,7 @@
         for f, (src, dst) in enumerate(((head_in, h), (cond_in, k))):
             row_copies.append((exists, source_exists, pltpu.make_async_remote_copy(
                 src_ref=src.at[:, mine],
-                dst_ref=dst.at[pl.ds(0, nz), ring, main],
+                dst_ref=dst.at[layers, ring, main],
                 send_sem=row_send.at[2 * i + f],
                 recv_sem=row_recv.at[2 * i + f],
                 device_id=(gx + dx, gy),
@@ -107,22 +123,15 @@
     local[1].wait()
     lane = lax.broadcasted_iota(jnp.int32, (1, LANES), 1)
 
-    def zero_tail(z, _):
-        h[z] = jnp.zeros((ring_rows, ring_cols), jnp.float32)
-        k[z] = jnp.zeros((ring_rows, ring_cols), jnp.float32)
-        return 0
-    lax.fori_loop(nz, h.shape[0], zero_tail, 0)
-
-    def pack(g, _):
+    per = LANES // SLOT
+    for g in range(groups):
         for f, src in enumerate((h, k)):
             total = jnp.zeros((tile_rows, LANES), jnp.float32)
-            for s in range(LANES // SLOT):
-                edge = pltpu.roll(src[g * (LANES // SLOT) + s, 0:tile_rows, 0:LANES], (HALO + SLOT * s) % LANES, 1)
+            for s in range(min(per, nz - g * per)):
+                edge = pltpu.roll(src[1 + g * per + s, 0:tile_rows, 0:LANES], (HALO + SLOT * s) % LANES, 1)
                 inside = (lane >= SLOT * s) & (lane < SLOT * (s + 1))
                 total = jnp.where(inside, edge, total)
             packed[f, g] = total
-        return 0
-    lax.fori_loop(0, groups, pack, 0)
 
     pack_copies = []
     n = 0
@@ -203,47 +212,76 @@
     for _, source, copy in row_copies + pack_copies:
         when(source, copy.wait_recv)
 
-    def unpack(g, _):
+    side_on_grid = on_grid[:, LANES:]
+    for g in range(groups):
         for f, dst in enumerate((h, k)):
             comb = jnp.where((lane % SLOT) < HALO, land_l[f, g], land_r[f, g])
-            for s in range(LANES // SLOT):
-                z = g * (LANES // SLOT) + s
+            for s in range(min(per, nz - g * per)):
                 side = pltpu.roll(comb, (LANES - HALO - SLOT * s) % LANES, 1)
-                full = jnp.concatenate([dst[z, :, 0:LANES], side], axis=1)
-                dst[z] = jnp.where(on_grid, full, 0.0)
+                dst[1 + g * per + s, :, LANES:] = jnp.where(side_on_grid, side, 0.0)
+
+    scale = 0.5 * flow_rate
+    masked = scale * mask
+
+    def east(x):
+        return pltpu.roll(x, ring_cols - 1, 1)
+
+    def west(x):
+        return pltpu.roll(x, 1, 1)
+
+    def south(x):
+        return pltpu.roll(x, ring_rows - 1, 0)
+
+    def north(x):
+        return pltpu.roll(x, 1, 0)
+
+    w_v[0] = empty
+
+    def weights(block, _):
+        z0 = block * BLOCK
+        here = k[z0 + 1]
+        up = jnp.where(z0 > 0, scale, 0.0) * (k[z0] + here)
+        for j in range(BLOCK):
+            z = z0 + j
+            after = k[z + 2]
+            down = jnp.where(z < nz - 1, scale, 0.0) * (here + after)
+            parts = [masked * (here + turn(here)) for turn in (east, west, south, north)]
+            for ref, part in zip((w_e, w_w, w_s, w_n), parts):
+                ref[z] = part
+            w_v[z + 1] = down
+            w_d[z] = 1.0 - ((parts[0] + parts[1]) + (parts[2] + parts[3]) + (up + down))
+            here, up = after, down
         return 0
-    lax.fori_loop(0, groups, unpack, 0)
-
-    scale = 0.5 * flow_rate
-
-    def weights(z, here):
-        after = k[z + 1]
-        w_e[z] = scale * (here + pltpu.roll(here, ring_cols - 1, 1))
-        w_s[z] = scale * (here + pltpu.roll(here, ring_rows - 1, 0))
-        w_v[z] = jnp.where(z < nz - 1, scale, 0.0) * (here + after)
-        return after
-    lax.fori_loop(0, nz, weights, k[0])
-
-    def step(cells, z, carry, last):
-        here, f_up = carry
-        f_e = w_e[z] * (pltpu.roll(here, ring_cols - 1, 1) - here)
-        f_s = w_s[z] * (pltpu.roll(here, ring_rows - 1, 0) - here)
-        if last:
-            after, f_v = here, jnp.zeros_like(here)
-        else:
-            after = cells[z + 1]
-            f_v = w_v[z] * (after - here)
-        change = (f_e - pltpu.roll(f_e, 1, 1)) + (f_s - pltpu.roll(f_s, 1, 0)) + (f_v - f_up)
-        cells[z] = here + mask * change
-        return after, f_v
-
-    zeros = jnp.zeros((ring_rows, ring_cols), jnp.float32)
-
-    def base_sweep(_, c):
-        carry = lax.fori_loop(0, nz - 1, lambda z, carry: step(h, z, carry, False), (h[0], zeros))
-        step(h, nz - 1, carry, True)
-        return c
-    lax.fori_loop(0, SWEEPS, base_sweep, 0)
+    lax.fori_loop(0, nz // BLOCK, weights, 0)
+
+    def step(src, z0, count):
+        before, here = src[z0], src[z0 + 1]
+        out = []
+        for j in range(count):
+            z = z0 + j
+            after = src[z + 2]
+            out.append(
+                (w_d[z] * here + w_e[z] * east(here))
+                + (w_w[z] * west(here) + w_s[z] * south(here))
+                + (w_n[z] * north(here) + (w_v[z] * before + w_v[z + 1] * after))
+            )
+            before, here = here, after
+        return out
+
+    def sweep(src, dst, last):
+        def body(block, _):
+            z0 = block * BLOCK
+            for j, new in enumerate(step(src, z0, BLOCK)):
+                if last:
+                    field[z0 + j] = new[0:tile_rows, 0:LANES]
+                else:
+                    dst[z0 + j + 1] = new
+            return 0
+        lax.fori_loop(0, nz // BLOCK, body, 0)
+
+    for n in range(SWEEPS):
+        src, dst = (h, h2) if n % 2 == 0 else (h2, h)
+        sweep(src, dst, n == SWEEPS - 1)
 
     for _, source, _, arrived in rech_copies:
         when(source, arrived.wait_recv)
@@ -260,16 +298,19 @@
     right = tile_sum(jnp.minimum(gy + 1, cols_n - 1))
     left = tile_sum(jnp.maximum(gy - 1, 0))
     side = jnp.where(lane < LANES // 2, right, left)
-    delta[0] = jnp.where(on_grid, jnp.concatenate([centre, side], axis=1), 0.0)
-    for z in range(1, SWEEPS + 2):
-        delta[z] = zeros
-    for sweep in range(SWEEPS):
-        reach = min(sweep + 2, nz)
-        lax.fori_loop(0, reach, lambda z, carry: step(delta, z, carry, False), (delta[0], zeros))
-    for z in range(min(SWEEPS + 1, nz)):
-        h[z, 0:tile_rows, 0:LANES] = h[z, 0:tile_rows, 0:LANES] + delta[z, 0:tile_rows, 0:LANES]
-
-    surf[gy] = h[0, 0:tile_rows, 0:LANES]
+    for z in range(SWEEPS + 3):
+        delta[z] = empty
+        delta2[z] = empty
+    delta[1] = jnp.where(on_grid, jnp.concatenate([centre, side], axis=1), 0.0)
+    for n in range(SWEEPS):
+        src, dst = (delta, delta2) if n % 2 == 0 else (delta2, delta)
+        for z, new in enumerate(step(src, 0, min(n + 2, nz))):
+            if n < SWEEPS - 1:
+                dst[z + 1] = new
+            else:
+                field[z] = field[z] + new[0:tile_rows, 0:LANES]
+
+    surf[gy] = field[0]
     surf_copies = []
     for dy in range(1, cols_n):
         to = lax.rem(gy + dy, cols_n)
@@ -287,7 +328,7 @@
         ]
         pair[0].start()
         surf_copies.append(pair)
-    field_copy = pltpu.make_async_copy(h.at[pl.ds(0, nz), whole, main], field_out, out_sem.at[1])
+    field_copy = pltpu.make_async_copy(field, field_out, out_sem.at[1])
     field_copy.start()
     for _, arrived in surf_copies:
         arrived.wait_recv()
@@ -382,12 +423,18 @@
         in_specs=[hbm] * 7 + [smem],
         out_specs=(hbm,) * 3,
         scratch_shapes=[
-            pltpu.VMEM((groups * per,) + ring, f32),
-            pltpu.VMEM((groups * per,) + ring, f32),
+            pltpu.VMEM((nz + 2,) + ring, f32),
+            pltpu.VMEM((nz + 2,) + ring, f32),
+            pltpu.VMEM((nz + 2,) + ring, f32),
+            pltpu.VMEM((nz, tile_rows, LANES), f32),
             pltpu.VMEM((nz,) + ring, f32),
             pltpu.VMEM((nz,) + ring, f32),
             pltpu.VMEM((nz,) + ring, f32),
-            pltpu.VMEM((SWEEPS + 2,) + ring, f32),
+            pltpu.VMEM((nz,) + ring, f32),
+            pltpu.VMEM((nz,) + ring, f32),
+            pltpu.VMEM((nz + 1,) + ring, f32),
+            pltpu.VMEM((SWEEPS + 3,) + ring, f32),
+            pltpu.VMEM((SWEEPS + 3,) + ring, f32),
             pltpu.VMEM((2, groups, tile_rows, LANES), f32),
             pltpu.VMEM((2, groups, ring[0], LANES), f32),
             pltpu.VMEM((2, groups, ring[0], LANES), f32),

time: 77.6 us -> 33.9 us (0.44)
  Pallas kernels: 75.9 us -> 32.1 us
    pallas_call x1, Pallas kernels: 73 us -> 29.3 us  [local(): pl.pallas_call(functools.partial(flow_kernel, (rows_n, cols_n, nz, tile_r...]
where the time goes in v3:
time: 33.9 us; the launch traced here: 33.4 us
  Pallas kernels  32.1 us (95%)
  between operations  1.29 us (4%)
    pallas_call x1, Pallas kernels, local(): pl.pallas_call(functools.partial(flow_kernel, (rows_n, cols_n, nz, tile_r...  29.3 us
    pallas_call x1, Pallas kernels, local(): pl.pallas_call(functools.partial(exchange_kernel, tile_rows, cols_n), nam...  2.84 us

profile of v3, /device:TPU:9, one launch (start us, length us, event | category | flops | bytes accessed | tf_op | source)
XLA Modules:
  0.0 33.4 jit_solution(3262925135378036893)
XLA Ops:
  1.3 29.3 %flow.1 = (f32[50,16,128]{2,1,0:T(8,128)}, f32[20,64,128]{2,1,0:T(8,128)}, f32[2,16,128]{2,1,0:T(8,128)}) custom-call(f32[20,64,128]{2,1,0:T(8,128)} %bitcast.6, f32[20,64,128]{2,1,0:T(8,128)} %bitcast.7, f32[64,128]{1,0:T(8,128)} %rain_in.1, f32[50,16,128]{2,1,0:T(8,128)} %head_in.1, f32[50,16,128]{2,1,0:T(8,128)} %cond_in.1, s32[1,64]{1,0:T(1,128)} %bitcast.8, ...), custom_call_target="tpu_custom_call" | custom-call | tf_op jit(solution)/shard_map/flow/pallas_call | solution.py:415
  30.6 2.8 %exchange.1 = (f32[50,16,128]{2,1,0:T(8,128)}, f32[20,64,128]{2,1,0:T(8,128)}, f32[8,128]{1,0:T(8,128)}) custom-call(f32[50,16,128]{2,1,0:T(8,128)} %get-tuple-element.9.field_in, f32[20,64,128]{2,1,0:T(8,128)} %get-tuple-element.10.wet_in, f32[2,16,128]{2,1,0:T(8,128)} %get-tuple-element.11.surf_in, s32[1,64]{1,0:T(1,128)} %bitcast.9, s32[1,64]{1,0:T(1,128)} %bitcast.11, ...), custom_call_target="tpu_custom_call" | custom-call | tf_op jit(solution)/shard_map/exchange/pallas_call | solution.py:456

commit v4 on v3

--- a/solution.py
+++ b/solution.py
@@ -11,6 +11,8 @@
 SWEEPS = 6
 HALO = 8
 BLOCK = 5
+CHUNK = 2 * BLOCK
+PAD = 8
 SLOT = 2 * HALO
 LANES = 128
 MESH = pl.DeviceIdType.MESH
@@ -49,7 +51,8 @@
     last = pl.ds(tile_rows - HALO, HALO)
     whole = pl.ds(0, tile_rows)
     main = pl.ds(0, LANES)
-    layers = pl.ds(1, nz)
+    layers = pl.ds(PAD, nz)
+    chunks = nz // CHUNK
 
     local = [
         pltpu.make_async_copy(src, dst, local_sem.at[i])
@@ -83,16 +86,18 @@
         return b if a is None else jnp.logical_and(a, b)
 
     empty = jnp.zeros((ring_rows, ring_cols), jnp.float32)
-    for ref in (h, h2, k):
-        ref[0] = empty
-        ref[nz + 1] = empty
+    for z in range(PAD):
+        for ref in (h, h2, k, w_d, w_e, w_w, w_s, w_n, w_v):
+            ref[z] = empty
+        for ref in (h, h2, k):
+            ref[PAD + nz + z] = empty
 
     def clear(rows):
         def body(z, _):
             for ref in (h, k):
                 ref[z, rows, main] = jnp.zeros((HALO, LANES), jnp.float32)
             return 0
-        lax.fori_loop(1, nz + 1, body, 0)
+        lax.fori_loop(PAD, PAD + nz, body, 0)
     pl.when(gx == 0)(lambda: clear(above))
     pl.when(gx == rows_n - 1)(lambda: clear(below))
 
@@ -101,23 +106,6 @@
         def greet(dx=dx, col=col):
             pl.semaphore_signal(barrier, inc=1, device_id=(gx + dx, col), device_id_type=MESH)
         when(exists, greet)
-    near_rows = 1 + has_below.astype(jnp.int32) + has_above.astype(jnp.int32)
-    pl.semaphore_wait(barrier, cols_n * near_rows - 1)
-
-    row_copies = []
-    for i, (dx, exists, ring, mine) in enumerate(row_steps[1:]):
-        source_exists = has_above if dx == 1 else has_below
-        for f, (src, dst) in enumerate(((head_in, h), (cond_in, k))):
-            row_copies.append((exists, source_exists, pltpu.make_async_remote_copy(
-                src_ref=src.at[:, mine],
-                dst_ref=dst.at[layers, ring, main],
-                send_sem=row_send.at[2 * i + f],
-                recv_sem=row_recv.at[2 * i + f],
-                device_id=(gx + dx, gy),
-                device_id_type=MESH,
-            )))
-    for exists, _, copy in row_copies:
-        when(exists, copy.start)
 
     local[0].wait()
     local[1].wait()
@@ -128,10 +116,38 @@
         for f, src in enumerate((h, k)):
             total = jnp.zeros((tile_rows, LANES), jnp.float32)
             for s in range(min(per, nz - g * per)):
-                edge = pltpu.roll(src[1 + g * per + s, 0:tile_rows, 0:LANES], (HALO + SLOT * s) % LANES, 1)
+                edge = pltpu.roll(src[PAD + g * per + s, 0:tile_rows, 0:LANES], (HALO + SLOT * s) % LANES, 1)
                 inside = (lane >= SLOT * s) & (lane < SLOT * (s + 1))
                 total = jnp.where(inside, edge, total)
             packed[f, g] = total
+
+    def row_copy(i, f, c):
+        dx, _, ring, mine = row_steps[1 + i]
+        src, dst = ((head_in, h), (cond_in, k))[f]
+        return pltpu.make_async_remote_copy(
+            src_ref=src.at[pl.ds(CHUNK * c, CHUNK), mine],
+            dst_ref=dst.at[pl.ds(PAD + CHUNK * c, CHUNK), ring, main],
+            send_sem=row_send.at[2 * i + f, c],
+            recv_sem=row_recv.at[2 * i + f, c],
+            device_id=(gx + dx, gy),
+            device_id_type=MESH,
+        )
+
+    def each_row(cond_of, c, act):
+        for i in range(2):
+            def body(i=i):
+                for f in (1, 0):
+                    act(row_copy(i, f, c))
+            pl.when(cond_of[i])(body)
+    sends_row, gets_row = (has_below, has_above), (has_above, has_below)
+
+    def start_rows(c, _):
+        each_row(sends_row, c, lambda copy: copy.start())
+        return 0
+
+    def finish_rows(c, _):
+        each_row(sends_row, c, lambda copy: copy.wait_send())
+        return 0
 
     pack_copies = []
     n = 0
@@ -147,8 +163,11 @@
                 device_id_type=MESH,
             )))
             n += 1
+    near_rows = 1 + has_below.astype(jnp.int32) + has_above.astype(jnp.int32)
+    pl.semaphore_wait(barrier, cols_n * near_rows - 1)
     for exists, _, copy in pack_copies:
         when(exists, copy.start)
+    lax.fori_loop(0, chunks, start_rows, 0)
 
     for copy in local[2:]:
         copy.wait()
@@ -209,7 +228,7 @@
     mask = (row_ok & col_ok).astype(jnp.float32)
     on_grid = mask > 0.0
 
-    for _, source, copy in row_copies + pack_copies:
+    for _, source, copy in pack_copies:
         when(source, copy.wait_recv)
 
     side_on_grid = on_grid[:, LANES:]
@@ -218,7 +237,7 @@
             comb = jnp.where((lane % SLOT) < HALO, land_l[f, g], land_r[f, g])
             for s in range(min(per, nz - g * per)):
                 side = pltpu.roll(comb, (LANES - HALO - SLOT * s) % LANES, 1)
-                dst[1 + g * per + s, :, LANES:] = jnp.where(side_on_grid, side, 0.0)
+                dst[PAD + g * per + s, :, LANES:] = jnp.where(side_on_grid, side, 0.0)
 
     scale = 0.5 * flow_rate
     masked = scale * mask
@@ -235,53 +254,60 @@
     def north(x):
         return pltpu.roll(x, 1, 0)
 
-    w_v[0] = empty
-
-    def weights(block, _):
-        z0 = block * BLOCK
-        here = k[z0 + 1]
-        up = jnp.where(z0 > 0, scale, 0.0) * (k[z0] + here)
+    def weights(z0):
+        here = k[PAD + z0]
+        up = jnp.where((z0 > 0) & (z0 < nz), scale, 0.0) * (k[PAD + z0 - 1] + here)
         for j in range(BLOCK):
             z = z0 + j
-            after = k[z + 2]
-            down = jnp.where(z < nz - 1, scale, 0.0) * (here + after)
+            at = PAD + z
+            after = k[at + 1]
+            down = jnp.where((z >= 0) & (z < nz - 1), scale, 0.0) * (here + after)
             parts = [masked * (here + turn(here)) for turn in (east, west, south, north)]
             for ref, part in zip((w_e, w_w, w_s, w_n), parts):
-                ref[z] = part
-            w_v[z + 1] = down
-            w_d[z] = 1.0 - ((parts[0] + parts[1]) + (parts[2] + parts[3]) + (up + down))
+                ref[at] = part
+            w_v[at + 1] = down
+            w_d[at] = 1.0 - ((parts[0] + parts[1]) + (parts[2] + parts[3]) + (up + down))
             here, up = after, down
-        return 0
-    lax.fori_loop(0, nz // BLOCK, weights, 0)
-
-    def step(src, z0, count):
-        before, here = src[z0], src[z0 + 1]
+
+    def step(src, at, w_at, count):
+        before, here = src[at - 1], src[at]
         out = []
         for j in range(count):
-            z = z0 + j
-            after = src[z + 2]
+            w = w_at + j
+            after = src[at + j + 1]
             out.append(
-                (w_d[z] * here + w_e[z] * east(here))
-                + (w_w[z] * west(here) + w_s[z] * south(here))
-                + (w_n[z] * north(here) + (w_v[z] * before + w_v[z + 1] * after))
+                (w_d[w] * here + w_e[w] * east(here))
+                + (w_w[w] * west(here) + w_s[w] * south(here))
+                + (w_n[w] * north(here) + (w_v[w] * before + w_v[w + 1] * after))
             )
             before, here = here, after
         return out
 
-    def sweep(src, dst, last):
-        def body(block, _):
-            z0 = block * BLOCK
-            for j, new in enumerate(step(src, z0, BLOCK)):
-                if last:
-                    field[z0 + j] = new[0:tile_rows, 0:LANES]
-                else:
-                    dst[z0 + j + 1] = new
-            return 0
-        lax.fori_loop(0, nz // BLOCK, body, 0)
-
-    for n in range(SWEEPS):
+    def sweep(n, z0):
         src, dst = (h, h2) if n % 2 == 0 else (h2, h)
-        sweep(src, dst, n == SWEEPS - 1)
+        for j, new in enumerate(step(src, PAD + z0, PAD + z0, BLOCK)):
+            if n < SWEEPS - 1:
+                dst[PAD + z0 + j] = new
+            else:
+                field[PAD + z0 + j] = new[0:tile_rows, 0:LANES]
+
+    def wave(c, _):
+        @pl.when(c < chunks)
+        def _():
+            each_row(gets_row, c, lambda copy: copy.wait_recv())
+
+        def run(start, work):
+            begin = jnp.where(start + BLOCK <= 0, 1, 0)
+            end = jnp.where(start + BLOCK >= nz, 1, 2)
+            def body(b, _):
+                work(start + BLOCK * b)
+                return 0
+            lax.fori_loop(begin, end, body, 0)
+        run(CHUNK * c - 1, weights)
+        for n in range(SWEEPS):
+            run(CHUNK * c - (n + 1), functools.partial(sweep, n))
+        return 0
+    lax.fori_loop(0, chunks + 1, wave, 0)
 
     for _, source, _, arrived in rech_copies:
         when(source, arrived.wait_recv)
@@ -304,13 +330,13 @@
     delta[1] = jnp.where(on_grid, jnp.concatenate([centre, side], axis=1), 0.0)
     for n in range(SWEEPS):
         src, dst = (delta, delta2) if n % 2 == 0 else (delta2, delta)
-        for z, new in enumerate(step(src, 0, min(n + 2, nz))):
+        for z, new in enumerate(step(src, 1, PAD, min(n + 2, nz))):
             if n < SWEEPS - 1:
                 dst[z + 1] = new
             else:
-                field[z] = field[z] + new[0:tile_rows, 0:LANES]
-
-    surf[gy] = field[0]
+                field[PAD + z] = field[PAD + z] + new[0:tile_rows, 0:LANES]
+
+    surf[gy] = field[PAD]
     surf_copies = []
     for dy in range(1, cols_n):
         to = lax.rem(gy + dy, cols_n)
@@ -328,14 +354,15 @@
         ]
         pair[0].start()
         surf_copies.append(pair)
-    field_copy = pltpu.make_async_copy(field, field_out, out_sem.at[1])
+    field_copy = pltpu.make_async_copy(field.at[layers], field_out, out_sem.at[1])
     field_copy.start()
     for _, arrived in surf_copies:
         arrived.wait_recv()
     surf_copy = pltpu.make_async_copy(surf, surf_out, out_sem.at[2])
     surf_copy.start()
 
-    for exists, _, copy in row_copies + pack_copies:
+    lax.fori_loop(0, chunks, finish_rows, 0)
+    for exists, _, copy in pack_copies:
         when(exists, copy.wait_send)
     for exists, _, out, _ in rech_copies:
         when(exists, out.wait_send)
@@ -423,16 +450,16 @@
         in_specs=[hbm] * 7 + [smem],
         out_specs=(hbm,) * 3,
         scratch_shapes=[
-            pltpu.VMEM((nz + 2,) + ring, f32),
-            pltpu.VMEM((nz + 2,) + ring, f32),
-            pltpu.VMEM((nz + 2,) + ring, f32),
-            pltpu.VMEM((nz, tile_rows, LANES), f32),
-            pltpu.VMEM((nz,) + ring, f32),
-            pltpu.VMEM((nz,) + ring, f32),
-            pltpu.VMEM((nz,) + ring, f32),
-            pltpu.VMEM((nz,) + ring, f32),
-            pltpu.VMEM((nz,) + ring, f32),
-            pltpu.VMEM((nz + 1,) + ring, f32),
+            pltpu.VMEM((nz + 2 * PAD,) + ring, f32),
+            pltpu.VMEM((nz + 2 * PAD,) + ring, f32),
+            pltpu.VMEM((nz + 2 * PAD,) + ring, f32),
+            pltpu.VMEM((nz + 2 * PAD, tile_rows, LANES), f32),
+            pltpu.VMEM((nz + 2 * PAD,) + ring, f32),
+            pltpu.VMEM((nz + 2 * PAD,) + ring, f32),
+            pltpu.VMEM((nz + 2 * PAD,) + ring, f32),
+            pltpu.VMEM((nz + 2 * PAD,) + ring, f32),
+            pltpu.VMEM((nz + 2 * PAD,) + ring, f32),
+            pltpu.VMEM((nz + 2 * PAD,) + ring, f32),
             pltpu.VMEM((SWEEPS + 3,) + ring, f32),
             pltpu.VMEM((SWEEPS + 3,) + ring, f32),
             pltpu.VMEM((2, groups, tile_rows, LANES), f32),
@@ -446,7 +473,7 @@
             pltpu.VMEM((1, blocks), jnp.int32),
             pltpu.VMEM((3, cols_n, cols_n, tile_rows, LANES), f32),
             pltpu.VMEM((cols_n, tile_rows, LANES), f32),
-            dma((7,)), dma((3,)), dma((4,)), dma((4,)), dma((6,)), dma((6,)),
+            dma((7,)), dma((3,)), dma((4, nz // CHUNK)), dma((4, nz // CHUNK)), dma((6,)), dma((6,)),
             dma((rech,)), dma((rech,)), dma((cols_n,)), dma((cols_n,)),
         ],
         compiler_params=pltpu.CompilerParams(

time: 33.9 us -> 32.6 us (0.962)
  the two profiles are of different devices: /device:TPU:9 before, /device:TPU:0 now
where the time goes in v4:
time: 32.6 us; the launch traced here: 32.4 us
  Pallas kernels  31.1 us (95%)
  between operations  1.29 us (4%)
    pallas_call x1, Pallas kernels, local(): pl.pallas_call(functools.partial(flow_kernel, (rows_n, cols_n, nz, tile_r...  28.3 us
    pallas_call x1, Pallas kernels, local(): pl.pallas_call(functools.partial(exchange_kernel, tile_rows, cols_n), nam...  2.84 us

profile of v4, /device:TPU:0, one launch (start us, length us, event | category | flops | bytes accessed | tf_op | source)
XLA Modules:
  0.0 32.4 jit_solution(11361543742902005536)
XLA Ops:
  1.3 28.3 %flow.1 = (f32[50,16,128]{2,1,0:T(8,128)}, f32[20,64,128]{2,1,0:T(8,128)}, f32[2,16,128]{2,1,0:T(8,128)}) custom-call(f32[20,64,128]{2,1,0:T(8,128)} %bitcast.6, f32[20,64,128]{2,1,0:T(8,128)} %bitcast.7, f32[64,128]{1,0:T(8,128)} %rain_in.1, f32[50,16,128]{2,1,0:T(8,128)} %head_in.1, f32[50,16,128]{2,1,0:T(8,128)} %cond_in.1, s32[1,64]{1,0:T(1,128)} %bitcast.8, ...), custom_call_target="tpu_custom_call" | custom-call | tf_op jit(solution)/shard_map/flow/pallas_call | solution.py:442
  29.6 2.8 %exchange.1 = (f32[50,16,128]{2,1,0:T(8,128)}, f32[20,64,128]{2,1,0:T(8,128)}, f32[8,128]{1,0:T(8,128)}) custom-call(f32[50,16,128]{2,1,0:T(8,128)} %get-tuple-element.9.field_in, f32[20,64,128]{2,1,0:T(8,128)} %get-tuple-element.10.wet_in, f32[2,16,128]{2,1,0:T(8,128)} %get-tuple-element.11.surf_in, s32[1,64]{1,0:T(1,128)} %bitcast.9, s32[1,64]{1,0:T(1,128)} %bitcast.11, ...), custom_call_target="tpu_custom_call" | custom-call | tf_op jit(solution)/shard_map/exchange/pallas_call | solution.py:483

commit v5 on v4

--- a/solution.py
+++ b/solution.py
@@ -33,7 +33,7 @@
     sizes,
     moist_in, diff_in, rain_in, head_in, cond_in, tile_in, offset_in, count_ref,
     field_out, wet_out, surf_out,
-    h, h2, k, field, w_d, w_e, w_w, w_s, w_n, w_v, delta, delta2, packed, land_l, land_r, moist, diff, ratio, rain,
+    h_land, k_land, spread, h, h2, k, field, w_d, w_e, w_w, w_s, w_n, w_v, delta, delta2, packed, land_l, land_r, moist, diff, ratio, rain,
     tile_ref, offset_ref, recharge, surf,
     local_sem, out_sem, row_send, row_recv, pack_send, pack_recv, rech_send, rech_recv,
     surf_send, surf_recv,
@@ -50,15 +50,14 @@
     first = pl.ds(0, HALO)
     last = pl.ds(tile_rows - HALO, HALO)
     whole = pl.ds(0, tile_rows)
-    main = pl.ds(0, LANES)
     layers = pl.ds(PAD, nz)
     chunks = nz // CHUNK
 
     local = [
         pltpu.make_async_copy(src, dst, local_sem.at[i])
         for i, (src, dst) in enumerate((
-            (head_in, h.at[layers, whole, main]),
-            (cond_in, k.at[layers, whole, main]),
+            (head_in, h_land.at[:, whole]),
+            (cond_in, k_land.at[:, whole]),
             (moist_in, moist),
             (diff_in, diff),
             (rain_in, rain),
@@ -94,10 +93,10 @@
 
     def clear(rows):
         def body(z, _):
-            for ref in (h, k):
-                ref[z, rows, main] = jnp.zeros((HALO, LANES), jnp.float32)
+            for ref in (h_land, k_land):
+                ref[z, rows] = jnp.zeros((HALO, LANES), jnp.float32)
             return 0
-        lax.fori_loop(PAD, PAD + nz, body, 0)
+        lax.fori_loop(0, nz, body, 0)
     pl.when(gx == 0)(lambda: clear(above))
     pl.when(gx == rows_n - 1)(lambda: clear(below))
 
@@ -113,20 +112,20 @@
 
     per = LANES // SLOT
     for g in range(groups):
-        for f, src in enumerate((h, k)):
+        for f, src in enumerate((h_land, k_land)):
             total = jnp.zeros((tile_rows, LANES), jnp.float32)
             for s in range(min(per, nz - g * per)):
-                edge = pltpu.roll(src[PAD + g * per + s, 0:tile_rows, 0:LANES], (HALO + SLOT * s) % LANES, 1)
+                edge = pltpu.roll(src[g * per + s, 0:tile_rows], (HALO + SLOT * s) % LANES, 1)
                 inside = (lane >= SLOT * s) & (lane < SLOT * (s + 1))
                 total = jnp.where(inside, edge, total)
             packed[f, g] = total
 
     def row_copy(i, f, c):
         dx, _, ring, mine = row_steps[1 + i]
-        src, dst = ((head_in, h), (cond_in, k))[f]
+        src, dst = ((head_in, h_land), (cond_in, k_land))[f]
         return pltpu.make_async_remote_copy(
             src_ref=src.at[pl.ds(CHUNK * c, CHUNK), mine],
-            dst_ref=dst.at[pl.ds(PAD + CHUNK * c, CHUNK), ring, main],
+            dst_ref=dst.at[pl.ds(CHUNK * c, CHUNK), ring],
             send_sem=row_send.at[2 * i + f, c],
             recv_sem=row_recv.at[2 * i + f, c],
             device_id=(gx + dx, gy),
@@ -221,7 +220,9 @@
     wet_copy = pltpu.make_async_copy(moist, wet_out, out_sem.at[0])
     wet_copy.start()
 
-    ring_row = lax.broadcasted_iota(jnp.int32, (ring_rows, ring_cols), 0)
+    slabs = ring_rows // 8
+    place = lax.broadcasted_iota(jnp.int32, (ring_rows, ring_cols), 0)
+    ring_row = slabs * (place % 8) + place // 8
     ring_col = lax.broadcasted_iota(jnp.int32, (ring_rows, ring_cols), 1)
     row_ok = (ring_row < tile_rows) | ((ring_row < tile_rows + HALO) & has_below) | ((ring_row >= tile_rows + HALO) & has_above)
     col_ok = (ring_col < LANES) | ((ring_col < LANES + LANES // 2) & has_right) | ((ring_col >= LANES + LANES // 2) & has_left)
@@ -231,10 +232,13 @@
     for _, source, copy in pack_copies:
         when(source, copy.wait_recv)
 
+    def interleaved(ref, *at):
+        return jnp.concatenate([ref[(*at, pl.ds(i, 8, stride=slabs))] for i in range(slabs)], axis=0)
+
     side_on_grid = on_grid[:, LANES:]
     for g in range(groups):
         for f, dst in enumerate((h, k)):
-            comb = jnp.where((lane % SLOT) < HALO, land_l[f, g], land_r[f, g])
+            comb = jnp.where((lane % SLOT) < HALO, interleaved(land_l, f, g), interleaved(land_r, f, g))
             for s in range(min(per, nz - g * per)):
                 side = pltpu.roll(comb, (LANES - HALO - SLOT * s) % LANES, 1)
                 dst[PAD + g * per + s, :, LANES:] = jnp.where(side_on_grid, side, 0.0)
@@ -249,10 +253,10 @@
         return pltpu.roll(x, 1, 1)
 
     def south(x):
-        return pltpu.roll(x, ring_rows - 1, 0)
+        return jnp.concatenate([x[8:], pltpu.roll(x[:8], 7, 0)], axis=0)
 
     def north(x):
-        return pltpu.roll(x, 1, 0)
+        return jnp.concatenate([pltpu.roll(x[-8:], 1, 0), x[:-8]], axis=0)
 
     def weights(z0):
         here = k[PAD + z0]
@@ -283,18 +287,30 @@
             before, here = here, after
         return out
 
+    tile_part = tile_rows // slabs
+
+    def put_tile(at, new, add):
+        for i in range(slabs):
+            rows = pl.ds(i, tile_part, stride=slabs)
+            part = new[8 * i : 8 * i + tile_part, 0:LANES]
+            field[at, rows] = field[at, rows] + part if add else part
+
     def sweep(n, z0):
         src, dst = (h, h2) if n % 2 == 0 else (h2, h)
         for j, new in enumerate(step(src, PAD + z0, PAD + z0, BLOCK)):
             if n < SWEEPS - 1:
                 dst[PAD + z0 + j] = new
             else:
-                field[PAD + z0 + j] = new[0:tile_rows, 0:LANES]
+                put_tile(PAD + z0 + j, new, False)
 
     def wave(c, _):
         @pl.when(c < chunks)
         def _():
             each_row(gets_row, c, lambda copy: copy.wait_recv())
+            for j in range(CHUNK):
+                z = CHUNK * c + j
+                for src, dst in ((h_land, h), (k_land, k)):
+                    dst[PAD + z, :, 0:LANES] = interleaved(src, z)
 
         def run(start, work):
             begin = jnp.where(start + BLOCK <= 0, 1, 0)
@@ -327,14 +343,17 @@
     for z in range(SWEEPS + 3):
         delta[z] = empty
         delta2[z] = empty
-    delta[1] = jnp.where(on_grid, jnp.concatenate([centre, side], axis=1), 0.0)
+    spread[0] = centre
+    spread[1] = side
+    start = jnp.concatenate([interleaved(spread, 0), interleaved(spread, 1)], axis=1)
+    delta[1] = jnp.where(on_grid, start, 0.0)
     for n in range(SWEEPS):
         src, dst = (delta, delta2) if n % 2 == 0 else (delta2, delta)
         for z, new in enumerate(step(src, 1, PAD, min(n + 2, nz))):
             if n < SWEEPS - 1:
                 dst[z + 1] = new
             else:
-                field[PAD + z] = field[PAD + z] + new[0:tile_rows, 0:LANES]
+                put_tile(PAD + z, new, True)
 
     surf[gy] = field[PAD]
     surf_copies = []
@@ -450,6 +469,9 @@
         in_specs=[hbm] * 7 + [smem],
         out_specs=(hbm,) * 3,
         scratch_shapes=[
+            pltpu.VMEM((nz, ring[0], LANES), f32),
+            pltpu.VMEM((nz, ring[0], LANES), f32),
+            pltpu.VMEM((2, ring[0], LANES), f32),
             pltpu.VMEM((nz + 2 * PAD,) + ring, f32),
             pltpu.VMEM((nz + 2 * PAD,) + ring, f32),
             pltpu.VMEM((nz + 2 * PAD,) + ring, f32),

time: 32.6 us -> 32.9 us (level)
  Pallas kernels: 31.1 us -> 31.5 us
    pallas_call x1, Pallas kernels: 28.3 us -> 28.6 us  [local(): pl.pallas_call(functools.partial(flow_kernel, (rows_n, cols_n, nz, tile_r...]
where the time goes in v5:
time: 32.9 us; the launch traced here: 32.8 us
  Pallas kernels  31.5 us (96%)
  between operations  1.29 us (4%)
    pallas_call x1, Pallas kernels, local(): pl.pallas_call(functools.partial(flow_kernel, (rows_n, cols_n, nz, tile_r...  28.6 us
    pallas_call x1, Pallas kernels, local(): pl.pallas_call(functools.partial(exchange_kernel, tile_rows, cols_n), nam...  2.84 us

profile of v5, /device:TPU:0, one launch (start us, length us, event | category | flops | bytes accessed | tf_op | source)
XLA Modules:
  0.0 32.8 jit_solution(5797143411943534886)
XLA Ops:
  1.3 28.6 %flow.1 = (f32[50,16,128]{2,1,0:T(8,128)}, f32[20,64,128]{2,1,0:T(8,128)}, f32[2,16,128]{2,1,0:T(8,128)}) custom-call(f32[20,64,128]{2,1,0:T(8,128)} %bitcast.6, f32[20,64,128]{2,1,0:T(8,128)} %bitcast.7, f32[64,128]{1,0:T(8,128)} %rain_in.1, f32[50,16,128]{2,1,0:T(8,128)} %head_in.1, f32[50,16,128]{2,1,0:T(8,128)} %cond_in.1, s32[1,64]{1,0:T(1,128)} %bitcast.8, ...), custom_call_target="tpu_custom_call" | custom-call | tf_op jit(solution)/shard_map/flow/pallas_call | solution.py:461
  29.9 2.8 %exchange.1 = (f32[50,16,128]{2,1,0:T(8,128)}, f32[20,64,128]{2,1,0:T(8,128)}, f32[8,128]{1,0:T(8,128)}) custom-call(f32[50,16,128]{2,1,0:T(8,128)} %get-tuple-element.9.field_in, f32[20,64,128]{2,1,0:T(8,128)} %get-tuple-element.10.wet_in, f32[2,16,128]{2,1,0:T(8,128)} %get-tuple-element.11.surf_in, s32[1,64]{1,0:T(1,128)} %bitcast.9, s32[1,64]{1,0:T(1,128)} %bitcast.11, ...), custom_call_target="tpu_custom_call" | custom-call | tf_op jit(solution)/shard_map/exchange/pallas_call | solution.py:505

commit v6 on v5

--- a/solution.py
+++ b/solution.py
@@ -10,9 +10,8 @@
 PATCH_DEV = 8
 SWEEPS = 6
 HALO = 8
-BLOCK = 5
-CHUNK = 2 * BLOCK
-PAD = 8
+CHUNK = 10
+PAD = CHUNK + 2
 SLOT = 2 * HALO
 LANES = 128
 MESH = pl.DeviceIdType.MESH
@@ -261,7 +260,7 @@
     def weights(z0):
         here = k[PAD + z0]
         up = jnp.where((z0 > 0) & (z0 < nz), scale, 0.0) * (k[PAD + z0 - 1] + here)
-        for j in range(BLOCK):
+        for j in range(CHUNK):
             z = z0 + j
             at = PAD + z
             after = k[at + 1]
@@ -297,7 +296,7 @@
 
     def sweep(n, z0):
         src, dst = (h, h2) if n % 2 == 0 else (h2, h)
-        for j, new in enumerate(step(src, PAD + z0, PAD + z0, BLOCK)):
+        for j, new in enumerate(step(src, PAD + z0, PAD + z0, CHUNK)):
             if n < SWEEPS - 1:
                 dst[PAD + z0 + j] = new
             else:
@@ -312,16 +311,9 @@
                 for src, dst in ((h_land, h), (k_land, k)):
                     dst[PAD + z, :, 0:LANES] = interleaved(src, z)
 
-        def run(start, work):
-            begin = jnp.where(start + BLOCK <= 0, 1, 0)
-            end = jnp.where(start + BLOCK >= nz, 1, 2)
-            def body(b, _):
-                work(start + BLOCK * b)
-                return 0
-            lax.fori_loop(begin, end, body, 0)
-        run(CHUNK * c - 1, weights)
+        weights(CHUNK * c - 1)
         for n in range(SWEEPS):
-            run(CHUNK * c - (n + 1), functools.partial(sweep, n))
+            sweep(n, CHUNK * c - (n + 1))
         return 0
     lax.fori_loop(0, chunks + 1, wave, 0)
 

time: 32.9 us -> 29.1 us (0.88)
  Pallas kernels: 31.5 us -> 27.6 us
    pallas_call x1, Pallas kernels: 28.6 us -> 24.8 us  [local(): pl.pallas_call(functools.partial(flow_kernel, (rows_n, cols_n, nz, tile_r...]
where the time goes in v6:
time: 29.1 us; the launch traced here: 28.9 us
  Pallas kernels  27.6 us (95%)
  between operations  1.29 us (4%)
    pallas_call x1, Pallas kernels, local(): pl.pallas_call(functools.partial(flow_kernel, (rows_n, cols_n, nz, tile_r...  24.8 us
    pallas_call x1, Pallas kernels, local(): pl.pallas_call(functools.partial(exchange_kernel, tile_rows, cols_n), nam...  2.84 us

profile of v6, /device:TPU:0, one launch (start us, length us, event | category | flops | bytes accessed | tf_op | source)
XLA Modules:
  0.0 28.9 jit_solution(6590016756713799435)
XLA Ops:
  1.3 24.8 %flow.1 = (f32[50,16,128]{2,1,0:T(8,128)}, f32[20,64,128]{2,1,0:T(8,128)}, f32[2,16,128]{2,1,0:T(8,128)}) custom-call(f32[20,64,128]{2,1,0:T(8,128)} %bitcast.6, f32[20,64,128]{2,1,0:T(8,128)} %bitcast.7, f32[64,128]{1,0:T(8,128)} %rain_in.1, f32[50,16,128]{2,1,0:T(8,128)} %head_in.1, f32[50,16,128]{2,1,0:T(8,128)} %cond_in.1, s32[1,64]{1,0:T(1,128)} %bitcast.8, ...), custom_call_target="tpu_custom_call" | custom-call | tf_op jit(solution)/shard_map/flow/pallas_call | solution.py:453
  26.1 2.8 %exchange.1 = (f32[50,16,128]{2,1,0:T(8,128)}, f32[20,64,128]{2,1,0:T(8,128)}, f32[8,128]{1,0:T(8,128)}) custom-call(f32[50,16,128]{2,1,0:T(8,128)} %get-tuple-element.9.field_in, f32[20,64,128]{2,1,0:T(8,128)} %get-tuple-element.10.wet_in, f32[2,16,128]{2,1,0:T(8,128)} %get-tuple-element.11.surf_in, s32[1,64]{1,0:T(1,128)} %bitcast.9, s32[1,64]{1,0:T(1,128)} %bitcast.11, ...), custom_call_target="tpu_custom_call" | custom-call | tf_op jit(solution)/shard_map/exchange/pallas_call | solution.py:497

commit v7 on v6

--- a/solution.py
+++ b/solution.py
@@ -183,7 +183,7 @@
         ratio[layer] = r
         moist[layer] = f
         return lower, r, f
-    lower, _, bottom = lax.fori_loop(1, depth, eliminate, (e0, r0, f0))
+    lower, _, bottom = lax.fori_loop(1, depth, eliminate, (e0, r0, f0), unroll=True)
     drain = lower * bottom
     hot = one_hot_rows(tile_ref[...], offset_ref[...], count_ref[0], cols_n, tile_rows)
     mine = jnp.dot(hot, drain, precision=lax.Precision.HIGHEST, preferred_element_type=jnp.float32)
@@ -215,7 +215,7 @@
         wet = moist[layer] + ratio[layer] * wet
         moist[layer] = wet
         return wet
-    lax.fori_loop(0, depth - 1, substitute, bottom)
+    lax.fori_loop(0, depth - 1, substitute, bottom, unroll=True)
     wet_copy = pltpu.make_async_copy(moist, wet_out, out_sem.at[0])
     wet_copy.start()
 
@@ -302,52 +302,6 @@
             else:
                 put_tile(PAD + z0 + j, new, False)
 
-    def wave(c, _):
-        @pl.when(c < chunks)
-        def _():
-            each_row(gets_row, c, lambda copy: copy.wait_recv())
-            for j in range(CHUNK):
-                z = CHUNK * c + j
-                for src, dst in ((h_land, h), (k_land, k)):
-                    dst[PAD + z, :, 0:LANES] = interleaved(src, z)
-
-        weights(CHUNK * c - 1)
-        for n in range(SWEEPS):
-            sweep(n, CHUNK * c - (n + 1))
-        return 0
-    lax.fori_loop(0, chunks + 1, wave, 0)
-
-    for _, source, _, arrived in rech_copies:
-        when(source, arrived.wait_recv)
-
-    def tile_sum(tile):
-        parts = []
-        for i, rows in ((0, whole), (1, last), (2, first)):
-            total = recharge[i, 0, tile, rows]
-            for s in range(1, cols_n):
-                total = total + recharge[i, s, tile, rows]
-            parts.append(total)
-        return jnp.concatenate([parts[0], parts[2], parts[1]], axis=0)
-    centre = tile_sum(gy)
-    right = tile_sum(jnp.minimum(gy + 1, cols_n - 1))
-    left = tile_sum(jnp.maximum(gy - 1, 0))
-    side = jnp.where(lane < LANES // 2, right, left)
-    for z in range(SWEEPS + 3):
-        delta[z] = empty
-        delta2[z] = empty
-    spread[0] = centre
-    spread[1] = side
-    start = jnp.concatenate([interleaved(spread, 0), interleaved(spread, 1)], axis=1)
-    delta[1] = jnp.where(on_grid, start, 0.0)
-    for n in range(SWEEPS):
-        src, dst = (delta, delta2) if n % 2 == 0 else (delta2, delta)
-        for z, new in enumerate(step(src, 1, PAD, min(n + 2, nz))):
-            if n < SWEEPS - 1:
-                dst[z + 1] = new
-            else:
-                put_tile(PAD + z, new, True)
-
-    surf[gy] = field[PAD]
     surf_copies = []
     for dy in range(1, cols_n):
         to = lax.rem(gy + dy, cols_n)
@@ -363,8 +317,58 @@
             )
             for slot in (gy, came)
         ]
-        pair[0].start()
         surf_copies.append(pair)
+
+    def finish_top():
+        for _, source, _, arrived in rech_copies:
+            when(source, arrived.wait_recv)
+
+        def tile_sum(tile):
+            parts = []
+            for i, rows in ((0, whole), (1, last), (2, first)):
+                total = recharge[i, 0, tile, rows]
+                for s in range(1, cols_n):
+                    total = total + recharge[i, s, tile, rows]
+                parts.append(total)
+            return jnp.concatenate([parts[0], parts[2], parts[1]], axis=0)
+        centre = tile_sum(gy)
+        right = tile_sum(jnp.minimum(gy + 1, cols_n - 1))
+        left = tile_sum(jnp.maximum(gy - 1, 0))
+        side = jnp.where(lane < LANES // 2, right, left)
+        for z in range(SWEEPS + 3):
+            delta[z] = empty
+            delta2[z] = empty
+        spread[0] = centre
+        spread[1] = side
+        start = jnp.concatenate([interleaved(spread, 0), interleaved(spread, 1)], axis=1)
+        delta[1] = jnp.where(on_grid, start, 0.0)
+        for n in range(SWEEPS):
+            src, dst = (delta, delta2) if n % 2 == 0 else (delta2, delta)
+            for z, new in enumerate(step(src, 1, PAD, min(n + 2, nz))):
+                if n < SWEEPS - 1:
+                    dst[z + 1] = new
+                else:
+                    put_tile(PAD + z, new, True)
+        surf[gy] = field[PAD]
+        for out, _ in surf_copies:
+            out.start()
+
+    def wave(c, _):
+        @pl.when(c < chunks)
+        def _():
+            each_row(gets_row, c, lambda copy: copy.wait_recv())
+            for j in range(CHUNK):
+                z = CHUNK * c + j
+                for src, dst in ((h_land, h), (k_land, k)):
+                    dst[PAD + z, :, 0:LANES] = interleaved(src, z)
+
+        weights(CHUNK * c - 1)
+        for n in range(SWEEPS):
+            sweep(n, CHUNK * c - (n + 1))
+        pl.when(c == 1)(finish_top)
+        return 0
+    lax.fori_loop(0, chunks + 1, wave, 0)
+
     field_copy = pltpu.make_async_copy(field.at[layers], field_out, out_sem.at[1])
     field_copy.start()
     for _, arrived in surf_copies:

time: 29.1 us -> 27.5 us (0.945)
  the two profiles are of different devices: /device:TPU:0 before, /device:TPU:9 now
where the time goes in v7:
time: 27.5 us; the launch traced here: 27.3 us
  Pallas kernels  26 us (95%)
  between operations  1.29 us (5%)
    pallas_call x1, Pallas kernels, local(): pl.pallas_call(functools.partial(flow_kernel, (rows_n, cols_n, nz, tile_r...  23.2 us
    pallas_call x1, Pallas kernels, local(): pl.pallas_call(functools.partial(exchange_kernel, tile_rows, cols_n), nam...  2.84 us

profile of v7, /device:TPU:9, one launch (start us, length us, event | category | flops | bytes accessed | tf_op | source)
XLA Modules:
  0.0 27.3 jit_solution(2364185064931115537)
XLA Ops:
  1.3 23.2 %flow.1 = (f32[50,16,128]{2,1,0:T(8,128)}, f32[20,64,128]{2,1,0:T(8,128)}, f32[2,16,128]{2,1,0:T(8,128)}) custom-call(f32[20,64,128]{2,1,0:T(8,128)} %bitcast.6, f32[20,64,128]{2,1,0:T(8,128)} %bitcast.7, f32[64,128]{1,0:T(8,128)} %rain_in.1, f32[50,16,128]{2,1,0:T(8,128)} %head_in.1, f32[50,16,128]{2,1,0:T(8,128)} %cond_in.1, s32[1,64]{1,0:T(1,128)} %bitcast.8, ...), custom_call_target="tpu_custom_call" | custom-call | tf_op jit(solution)/shard_map/flow/pallas_call | solution.py:457
  24.4 2.8 %exchange.1 = (f32[50,16,128]{2,1,0:T(8,128)}, f32[20,64,128]{2,1,0:T(8,128)}, f32[8,128]{1,0:T(8,128)}) custom-call(f32[50,16,128]{2,1,0:T(8,128)} %get-tuple-element.9.field_in, f32[20,64,128]{2,1,0:T(8,128)} %get-tuple-element.10.wet_in, f32[2,16,128]{2,1,0:T(8,128)} %get-tuple-element.11.surf_in, s32[1,64]{1,0:T(1,128)} %bitcast.9, s32[1,64]{1,0:T(1,128)} %bitcast.11, ...), custom_call_target="tpu_custom_call" | custom-call | tf_op jit(solution)/shard_map/exchange/pallas_call | solution.py:501

commit v8 on v7

--- a/solution.py
+++ b/solution.py
@@ -34,7 +34,7 @@
     field_out, wet_out, surf_out,
     h_land, k_land, spread, h, h2, k, field, w_d, w_e, w_w, w_s, w_n, w_v, delta, delta2, packed, land_l, land_r, moist, diff, ratio, rain,
     tile_ref, offset_ref, recharge, surf,
-    local_sem, out_sem, row_send, row_recv, pack_send, pack_recv, rech_send, rech_recv,
+    local_sem, out_sem, field_sem, row_send, row_recv, pack_send, pack_recv, rech_send, rech_recv,
     surf_send, surf_recv,
 ):
     rows_n, cols_n, nz, tile_rows = sizes
@@ -353,6 +353,11 @@
         for out, _ in surf_copies:
             out.start()
 
+    def field_copy(c):
+        return pltpu.make_async_copy(
+            field.at[pl.ds(PAD + CHUNK * c, CHUNK)], field_out.at[pl.ds(CHUNK * c, CHUNK)], field_sem.at[c]
+        )
+
     def wave(c, _):
         @pl.when(c < chunks)
         def _():
@@ -366,11 +371,11 @@
         for n in range(SWEEPS):
             sweep(n, CHUNK * c - (n + 1))
         pl.when(c == 1)(finish_top)
+        pl.when(c >= 2)(lambda: field_copy(c - 2).start())
         return 0
     lax.fori_loop(0, chunks + 1, wave, 0)
 
-    field_copy = pltpu.make_async_copy(field.at[layers], field_out, out_sem.at[1])
-    field_copy.start()
+    field_copy(chunks - 1).start()
     for _, arrived in surf_copies:
         arrived.wait_recv()
     surf_copy = pltpu.make_async_copy(surf, surf_out, out_sem.at[2])
@@ -384,7 +389,8 @@
     for out, _ in surf_copies:
         out.wait_send()
     wet_copy.wait()
-    field_copy.wait()
+    for c in range(chunks):
+        field_copy(c).wait()
     surf_copy.wait()
 
 
@@ -491,7 +497,7 @@
             pltpu.VMEM((1, blocks), jnp.int32),
             pltpu.VMEM((3, cols_n, cols_n, tile_rows, LANES), f32),
             pltpu.VMEM((cols_n, tile_rows, LANES), f32),
-            dma((7,)), dma((3,)), dma((4, nz // CHUNK)), dma((4, nz // CHUNK)), dma((6,)), dma((6,)),
+            dma((7,)), dma((3,)), dma((nz // CHUNK,)), dma((4, nz // CHUNK)), dma((4, nz // CHUNK)), dma((6,)), dma((6,)),
             dma((rech,)), dma((rech,)), dma((cols_n,)), dma((cols_n,)),
         ],
         compiler_params=pltpu.CompilerParams(

time: 27.5 us -> 27.4 us (level)
  no operation moved by 1% of the time
where the time goes in v8:
time: 27.4 us; the launch traced here: 27.3 us
  Pallas kernels  26 us (95%)
  between operations  1.29 us (5%)
    pallas_call x1, Pallas kernels, local(): pl.pallas_call(functools.partial(flow_kernel, (rows_n, cols_n, nz, tile_r...  23.1 us
    pallas_call x1, Pallas kernels, local(): pl.pallas_call(functools.partial(exchange_kernel, tile_rows, cols_n), nam...  2.84 us

profile of v8, /device:TPU:9, one launch (start us, length us, event | category | flops | bytes accessed | tf_op | source)
XLA Modules:
  0.0 27.3 jit_solution(14952459617660560272)
XLA Ops:
  1.3 23.1 %flow.1 = (f32[50,16,128]{2,1,0:T(8,128)}, f32[20,64,128]{2,1,0:T(8,128)}, f32[2,16,128]{2,1,0:T(8,128)}) custom-call(f32[20,64,128]{2,1,0:T(8,128)} %bitcast.6, f32[20,64,128]{2,1,0:T(8,128)} %bitcast.7, f32[64,128]{1,0:T(8,128)} %rain_in.1, f32[50,16,128]{2,1,0:T(8,128)} %head_in.1, f32[50,16,128]{2,1,0:T(8,128)} %cond_in.1, s32[1,64]{1,0:T(1,128)} %bitcast.8, ...), custom_call_target="tpu_custom_call" | custom-call | tf_op jit(solution)/shard_map/flow/pallas_call | solution.py:463
  24.4 2.8 %exchange.1 = (f32[50,16,128]{2,1,0:T(8,128)}, f32[20,64,128]{2,1,0:T(8,128)}, f32[8,128]{1,0:T(8,128)}) custom-call(f32[50,16,128]{2,1,0:T(8,128)} %get-tuple-element.9.field_in, f32[20,64,128]{2,1,0:T(8,128)} %get-tuple-element.10.wet_in, f32[2,16,128]{2,1,0:T(8,128)} %get-tuple-element.11.surf_in, s32[1,64]{1,0:T(1,128)} %bitcast.9, s32[1,64]{1,0:T(1,128)} %bitcast.11, ...), custom_call_target="tpu_custom_call" | custom-call | tf_op jit(solution)/shard_map/exchange/pallas_call | solution.py:507
